TPU v7x, 256 devices: a whole 4x4x8 slice. The times are simulated.
256 devices in a mesh: section: 8 (over z), ctx: 32 (over x, y, core).
Axes of the slice: x: 4, y: 4, z: 8, core: 2. Of those that a mesh axis runs over, the one named last changes fastest.
Arguments:
- queries: bfloat16 [8, 4096, 4096], P('section', 'ctx'), may hold values from -130 to 130
- keys_new: bfloat16 [8, 4096, 1024], P('section', 'ctx'), may hold values from -6 to 6
- values_new: bfloat16 [8, 4096, 1024], P('section', 'ctx'), may hold values from -6 to 6
- stretch_cache: bfloat16 [8, 2048, 2048], P('section'), may hold values from -6 to 6
- hadamard_signs: int32 [8, 2, 128], P('section'), may hold values from -1 to 1, as said below
- stretch_docs: int32 [32], replicated, may hold values from 0 to 7, never falling along the last dimension, each value on 1 to 17 neighbouring positions
Outputs:
- handed: bfloat16 [8, 4096, 4096], P('section', 'ctx')
Inputs may be any that keep to these rules, and one draw needn't show every extreme that they name: `hadamard_signs`: each entry is -1 or 1. `stretch_docs`: never falling along the stretches; each document covers 1 to 17 stretches in a row.
All inputs are finite; a program needn't handle non-finite values.
Results may differ from a plain program's by a relative error of at most 0.0099.
Values may be sent and summed in bfloat16 or wider, within the bound.
No kernel may reach another device: no remote copies, remote signals or barrier semaphores. Data moves between devices by JAX's collectives and lax.ppermute only.
A program may use at most 128 MiB of HBM per device.

v0:
```python
import math

import jax
import jax.numpy as jnp
import numpy as np
from jax import lax
from jax.sharding import PartitionSpec as P

CACHE = 256


def from_behind(block, axis, distance):
    devices = range(lax.axis_size(axis))
    route = [((i - distance) % len(devices), i) for i in devices]
    return lax.ppermute(block, axis, route)


def hadamard(length):
    numbers = np.arange(length)
    common = numbers[:, None] & numbers[None, :]
    parity = np.zeros((length, length), np.int64)
    for bit_place in range(max(int(length).bit_length(), 1)):
        parity = parity ^ common >> bit_place & 1
    return 1.0 - 2.0 * parity


def rotate(source, sign_row, rotation):
    row_count = source.shape[0]
    head_size = rotation.shape[0]
    shaped = (source.reshape(row_count, -1, head_size) * sign_row.astype(source.dtype)).reshape(
        -1, head_size
    )
    turned = jnp.dot(shaped, rotation, preferred_element_type=jnp.float32) * head_size ** (-0.5)
    return turned.reshape(row_count, -1).astype(jnp.bfloat16)


def attend(running, query_turned, key_rows, visible):
    row_max, row_sum, weighted = running
    kv_heads = query_turned.shape[1]
    head_size = query_turned.shape[3]
    key_part = key_rows[:, : kv_heads * head_size].reshape(-1, kv_heads, head_size)
    value_part = key_rows[:, kv_heads * head_size :].reshape(-1, kv_heads, head_size)
    scores = jnp.einsum(
        "rkgd,nkd->rkgn", query_turned, key_part, preferred_element_type=jnp.float32
    ) * head_size ** (-0.5)
    scores = jnp.where(visible[:, None, None, :], scores, -jnp.inf)
    new_max = jnp.maximum(row_max, scores.max(-1))
    factor = jnp.exp(row_max - new_max)
    exponent = jnp.exp(scores - new_max[..., None])
    row_sum = row_sum * factor + exponent.sum(-1)
    weighted = weighted * factor[..., None] + jnp.einsum(
        "rkgn,nkd->rkgd",
        exponent.astype(jnp.bfloat16),
        value_part,
        preferred_element_type=jnp.float32,
    )
    return (new_max, row_sum, weighted)


def attend_columns(running, query_turned, key_rows, allowed):
    visible = jnp.broadcast_to(allowed[None, :], (query_turned.shape[0], key_rows.shape[0]))
    return lax.cond(
        jnp.any(allowed),
        lambda state: attend(state, query_turned, key_rows, visible),
        lambda state: state,
        running,
    )


def doc_lookup(stretch_docs, stretch_ids, sources):
    return jnp.sum(
        jnp.where(sources[:, None] == stretch_ids[None, :], stretch_docs[None, :], 0), axis=1
    )


def per_device(queries, keys_new, values_new, stretch_cache, hadamard_signs, stretch_docs):
    head_size = hadamard_signs.shape[-1]
    rotation = jnp.asarray(hadamard(head_size), dtype=jnp.bfloat16)
    inverse = jnp.asarray(hadamard(head_size), dtype=jnp.float32)
    sign_keys = hadamard_signs[0, 0]
    sign_values = hadamard_signs[0, 1]
    query_rows = queries[0]
    row_total = query_rows.shape[0]
    kv_width = keys_new.shape[-1]
    kv_heads = kv_width // head_size
    groups = query_rows.shape[-1] // kv_width
    new_front = jnp.concatenate(
        [rotate(keys_new[0], sign_keys, rotation), rotate(values_new[0], sign_values, rotation)],
        axis=1,
    )
    query_turned = rotate(query_rows, sign_keys, rotation).reshape(
        row_total, kv_heads, groups, head_size
    )
    my_stretch = lax.axis_index("ctx")
    stretch_ids = jnp.arange(stretch_docs.shape[0], dtype=jnp.int32)
    my_doc = jnp.sum(jnp.where(stretch_ids == my_stretch, stretch_docs, 0))
    query_row = jnp.arange(row_total, dtype=jnp.int32)
    running = (
        jnp.full((row_total, kv_heads, groups), -jnp.inf, jnp.float32),
        jnp.zeros((row_total, kv_heads, groups), jnp.float32),
        jnp.zeros((row_total, kv_heads, groups, head_size), jnp.float32),
    )
    own_visible = query_row[None, :] <= query_row[:, None]
    running = attend(running, query_turned, new_front, own_visible)
    cache_rows = lax.dynamic_slice_in_dim(stretch_cache[0], my_doc * CACHE, CACHE, 0)
    cache_step_rows = math.gcd(cache_rows.shape[0], 512)
    cache_blocks = cache_rows.reshape(-1, cache_step_rows, cache_rows.shape[-1])
    full_visible = jnp.ones((row_total, cache_step_rows), dtype=bool)

    def cache_step(state, key_rows):
        return (attend(state, query_turned, key_rows, full_visible), None)

    running, _ = lax.scan(cache_step, running, cache_blocks)
    state = running
    portion = lax.all_gather(new_front, "ctx", axis=0, tiled=True)
    portion_rows = portion.shape[0]
    block_rows = math.gcd(portion_rows, 512)
    offsets = block_rows * jnp.arange(portion_rows // block_rows, dtype=jnp.int32)

    def inner_step(inner_state, item):
        key_rows, offset = item
        sources = (offset + jnp.arange(block_rows, dtype=jnp.int32)) // row_total
        allowed = (sources < my_stretch) & (
            doc_lookup(stretch_docs, stretch_ids, sources) == my_doc
        )
        return (attend_columns(inner_state, query_turned, key_rows, allowed), None)

    state, _ = lax.scan(
        inner_step, state, (portion.reshape(-1, block_rows, portion.shape[-1]), offsets)
    )
    running = state
    row_max, row_sum, weighted = running
    averaged = weighted / row_sum[..., None]
    restored = jnp.dot(averaged.reshape(-1, head_size), inverse, precision=lax.Precision.HIGHEST)
    restored = restored * head_size ** (-0.5) * sign_values.astype(jnp.float32)
    heads_out = restored.reshape(row_total, -1).astype(jnp.bfloat16)
    handed = from_behind(heads_out, "section", 1)
    return handed[None]


def solution(mesh):
    in_specs = (
        P("section", "ctx", None),
        P("section", "ctx", None),
        P("section", "ctx", None),
        P("section", None, None),
        P("section", None, None),
        P(),
    )
    out_specs = P("section", "ctx", None)
    return jax.shard_map(
        per_device, mesh=mesh, in_specs=in_specs, out_specs=out_specs, check_vma=False
    )
```

profile of v0, /device:TPU:26, one launch (start us, length us, event | category | flops | bytes accessed | tf_op | source)
XLA Modules:
  0.0 224.3 jit_solution(9531708934384979085)
XLA Ops:
  22.4 1.8 copy.61
  24.3 66.6 %all-gather.2.cloned.1.call-done = bf16[4096,2048]{1,0:T(8,128)(2,1)} async-done(((bf16[128,2048]{1,0:T(8,128)(2,1)}), bf16[4096,2048]{1,0:T(8,128)(2,1)}) %all-gather.2.cloned.1.call-update) | async-done | bytes 16777232 | tf_op jit(solution)/shard_map/all_gather | solution.py:115
  90.9 21.7 %copy.62 = bf16[8,512,2048]{1,2,0:T(8,128)(2,1)} copy(bf16[8,512,2048]{2,1,0:T(8,128)(2,1)} %bitcast.95) | data formatting | bytes 33554432
  112.7 72.5 %while.5 = (s32[]{:T(128)}, f32[128,8,4]{0,2,1:T(4,128)S(1)}, f32[128,8,4]{0,2,1:T(4,128)S(1)}, f32[128,8,4,128]{3,0,2,1:T(8,128)S(1)}, s32[8]{0:T(128)S(1)}, /*...) while((s32[]{:T(128)}, f32[128,8,4]{0,2,1:T(4,128)S(1)}, ...), condition=%wide.region_12.13_spmd.clone, body=%wide.region_5.12_spmd.clone.sunk | while | flops 1097944064 | bytes 41174472 | solution.py:128
  113.9 1.9 and_reduce_fusion.3
  116.5 10.5 %conditional.3 = ((f32[128,8,4]{0,2,1:T(4,128)S(1)}, f32[128,8,4]{0,2,1:T(4,128)S(1)}, f32[128,8,4,128]{3,0,2,1:T(8,128)S(1)})) conditional(s32[]{:T(128)} %convert_element_type.97, (f32[128,8,4]{0,2,1:T(4,128)S(1)}, f32[128,8,4]{0,2,1:T(4,128)S(1)}, f32[128,8,4,128]{3,0,2,1:T(8,128)S(1)}) %tuple.62, (s32[]{:T(128)}, s32[1,512]{1,0:T(1,128)S(1)}, ...), branch_computations={%region_8.8_spmd, %region_9.11_spmd.clone} | conditional | flops 1097876992 | bytes 41163828 | solution.py:62
  117.8 1.7 dynamic-slice_bitcast_fusion
  119.7 2.0 bitcast_reduce_fusion
  121.7 2.0 fusion.4
  123.8 3.1 %bitcast_add_fusion = f32[128,8,4,128]{3,0,2,1:T(8,128)S(1)} fusion(f32[128,8,4,128]{3,0,2,1:T(8,128)S(1)} %get-tuple-element.341, bf16[512,8,128,1]{0,2,3,1:T(8,128)(2,1)S(1)} %bitcast.94, f32[8,512,128,4]{2,1,3,0:T(8,128)S(1)} %get-tuple-element.451, f32[128,8,4]{0,2,1:T(4,128)S(1)} %max.17, pred[512]{0:T(512)(128)(4,1)S(1)} %and_reduce_fusion, ...), kind=kOutput, calls=%fused_computation.12 | convolution fusion | flops 546308096 | bytes 13664768 | tf_op jit(solution)/shard_map/while/body/eval_jaxpr/cond/branch_1_fun/rkgn,nkd->rkgd/dot_general | solution.py:51
  128.2 1.9 and_reduce_fusion.3
  130.7 10.5 %conditional.3 = ((f32[128,8,4]{0,2,1:T(4,128)S(1)}, f32[128,8,4]{0,2,1:T(4,128)S(1)}, f32[128,8,4,128]{3,0,2,1:T(8,128)S(1)})) conditional(s32[]{:T(128)} %convert_element_type.97, (f32[128,8,4]{0,2,1:T(4,128)S(1)}, f32[128,8,4]{0,2,1:T(4,128)S(1)}, f32[128,8,4,128]{3,0,2,1:T(8,128)S(1)}) %tuple.62, (s32[]{:T(128)}, s32[1,512]{1,0:T(1,128)S(1)}, ...), branch_computations={%region_8.8_spmd, %region_9.11_spmd.clone} | conditional | flops 1097876992 | bytes 41163828 | solution.py:62
  132.1 1.7 dynamic-slice_bitcast_fusion
  133.9 2.0 bitcast_reduce_fusion
  136.0 2.0 fusion.4
  138.0 3.1 %bitcast_add_fusion = f32[128,8,4,128]{3,0,2,1:T(8,128)S(1)} fusion(f32[128,8,4,128]{3,0,2,1:T(8,128)S(1)} %get-tuple-element.341, bf16[512,8,128,1]{0,2,3,1:T(8,128)(2,1)S(1)} %bitcast.94, f32[8,512,128,4]{2,1,3,0:T(8,128)S(1)} %get-tuple-element.451, f32[128,8,4]{0,2,1:T(4,128)S(1)} %max.17, pred[512]{0:T(512)(128)(4,1)S(1)} %and_reduce_fusion, ...), kind=kOutput, calls=%fused_computation.12 | convolution fusion | flops 546308096 | bytes 13664768 | tf_op jit(solution)/shard_map/while/body/eval_jaxpr/cond/branch_1_fun/rkgn,nkd->rkgd/dot_general | solution.py:51
  142.5 1.9 and_reduce_fusion.3
  145.0 10.5 %conditional.3 = ((f32[128,8,4]{0,2,1:T(4,128)S(1)}, f32[128,8,4]{0,2,1:T(4,128)S(1)}, f32[128,8,4,128]{3,0,2,1:T(8,128)S(1)})) conditional(s32[]{:T(128)} %convert_element_type.97, (f32[128,8,4]{0,2,1:T(4,128)S(1)}, f32[128,8,4]{0,2,1:T(4,128)S(1)}, f32[128,8,4,128]{3,0,2,1:T(8,128)S(1)}) %tuple.62, (s32[]{:T(128)}, s32[1,512]{1,0:T(1,128)S(1)}, ...), branch_computations={%region_8.8_spmd, %region_9.11_spmd.clone} | conditional | flops 1097876992 | bytes 41163828 | solution.py:62
  148.2 2.0 bitcast_reduce_fusion
  150.3 2.0 fusion.4
  152.3 3.1 %bitcast_add_fusion = f32[128,8,4,128]{3,0,2,1:T(8,128)S(1)} fusion(f32[128,8,4,128]{3,0,2,1:T(8,128)S(1)} %get-tuple-element.341, bf16[512,8,128,1]{0,2,3,1:T(8,128)(2,1)S(1)} %bitcast.94, f32[8,512,128,4]{2,1,3,0:T(8,128)S(1)} %get-tuple-element.451, f32[128,8,4]{0,2,1:T(4,128)S(1)} %max.17, pred[512]{0:T(512)(128)(4,1)S(1)} %and_reduce_fusion, ...), kind=kOutput, calls=%fused_computation.12 | convolution fusion | flops 546308096 | bytes 13664768 | tf_op jit(solution)/shard_map/while/body/eval_jaxpr/cond/branch_1_fun/rkgn,nkd->rkgd/dot_general | solution.py:51
  156.8 1.9 and_reduce_fusion.3
  159.3 10.5 %conditional.3 = ((f32[128,8,4]{0,2,1:T(4,128)S(1)}, f32[128,8,4]{0,2,1:T(4,128)S(1)}, f32[128,8,4,128]{3,0,2,1:T(8,128)S(1)})) conditional(s32[]{:T(128)} %convert_element_type.97, (f32[128,8,4]{0,2,1:T(4,128)S(1)}, f32[128,8,4]{0,2,1:T(4,128)S(1)}, f32[128,8,4,128]{3,0,2,1:T(8,128)S(1)}) %tuple.62, (s32[]{:T(128)}, s32[1,512]{1,0:T(1,128)S(1)}, ...), branch_computations={%region_8.8_spmd, %region_9.11_spmd.clone} | conditional | flops 1097876992 | bytes 41163828 | solution.py:62
  162.5 2.0 bitcast_reduce_fusion
  164.5 2.0 fusion.4
  166.6 3.1 %bitcast_add_fusion = f32[128,8,4,128]{3,0,2,1:T(8,128)S(1)} fusion(f32[128,8,4,128]{3,0,2,1:T(8,128)S(1)} %get-tuple-element.341, bf16[512,8,128,1]{0,2,3,1:T(8,128)(2,1)S(1)} %bitcast.94, f32[8,512,128,4]{2,1,3,0:T(8,128)S(1)} %get-tuple-element.451, f32[128,8,4]{0,2,1:T(4,128)S(1)} %max.17, pred[512]{0:T(512)(128)(4,1)S(1)} %and_reduce_fusion, ...), kind=kOutput, calls=%fused_computation.12 | convolution fusion | flops 546308096 | bytes 13664768 | tf_op jit(solution)/shard_map/while/body/eval_jaxpr/cond/branch_1_fun/rkgn,nkd->rkgd/dot_general | solution.py:51
  171.0 1.9 and_reduce_fusion.3
  174.9 1.9 and_reduce_fusion.3
  178.7 1.9 and_reduce_fusion.3
  182.6 1.9 and_reduce_fusion.3
  187.3 1.8 fusion.19
  191.2 25.3 %collective-permute-done = bf16[128,4096]{1,0:T(8,128)(2,1)S(1)} collective-permute-done((bf16[128,4096]{1,0:T(8,128)(2,1)S(1)}, bf16[128,4096]{1,0:T(8,128)(2,1)S(1)}, u32[]{:S(2)}, u32[]{:S(2)}) %collective-permute-start) | collective-permute-done | bytes 1048608 | tf_op jit(solution)/shard_map/ppermute | solution.py:15
  (108 shorter events, 39.5 us)
Async XLA Ops:
  6.5 4.6 %copy-start.1 = (bf16[128,128]{1,0:T(8,128)(2,1)S(1)}, bf16[128,128]{1,0:T(8,128)(2,1)}, u32[]{:S(2)}) copy-start(bf16[128,128]{1,0:T(8,128)(2,1)} %constant.109.clone) | copy-start | bytes 98308
  6.5 84.4 %all-gather.2.cloned.1.call-start = ((), (), s32[]{:S(2)}) async-start(), calls=%async_computation | async-start | bytes 17301504 | tf_op jit(solution)/shard_map/all_gather | solution.py:115
  9.0 3.4 %copy-start.3 = (s32[32]{0:T(128)S(1)}, s32[32]{0:T(128)}, u32[]{:S(2)}) copy-start(s32[32]{0:T(128)} %param.17) | copy-start | bytes 388
  22.4 1.9 copy-start.4
  90.9 21.7 %copy-start = (f32[128,8,4,128]{3,0,2,1:T(8,128)S(1)}, f32[128,8,4,128]{3,0,2,1:T(8,128)}, u32[]{:S(2)}) copy-start(f32[128,8,4,128]{3,0,2,1:T(8,128)} %copy.61) | copy-start | bytes 6291460
  185.9 1.4 copy-start.2
  189.5 27.0 %collective-permute-start = (bf16[128,4096]{1,0:T(8,128)(2,1)S(1)}, bf16[128,4096]{1,0:T(8,128)(2,1)S(1)}, u32[]{:S(2)}, u32[]{:S(2)}) collective-permute-start(bf16[128,4096]{1,0:T(8,128)(2,1)S(1)} %convert_element_type.79), channel_id=1, source_target_pairs={{224,0},{0,32},{32,64},{64,96},{96,128},{128,160},{160,192},{192,2... | collective-permute-start | bytes 3145736 | tf_op jit(solution)/shard_map/ppermute | solution.py:15
Sparse Core Ops, SparseCore 0:
  12.5 78.3 all-gather.1
where the time goes:
time: 227 us; the launch traced here: 224 us
  waiting for transfers between devices  92 us (41%)
  local copies, waits for them, and re-layouts  44.7 us (20%)
  other arithmetic  39 us (17%)
  matrix products  27.1 us (12%)
  between operations  14.3 us (6%)
  loops' own time  5.57 us (2%)
    all_gather x1, waiting for transfers between devices, per_device(): portion = lax.all_gather(new_front, 'ctx', axis=0, tiled=True)  66.6 us
    ppermute x1, waiting for transfers between devices, from_behind(): return lax.ppermute(block, axis, route)  25.3 us
    unnamed x13, local copies, waits for them, and re-layouts  24.6 us
    reduce_or x8, other arithmetic, attend_columns(): jnp.any(allowed)  15.4 us
    dot_general x6, matrix products, attend(): jnp.einsum('rkgn,nkd->rkgd', exponent.astype(jnp.bfloat16), value_part, p...  14.2 us
    dot_general x6, matrix products, attend(): jnp.einsum('rkgd,nkd->rkgn', query_turned, key_part, preferred_element_ty...  9.6 us
    reduce_sum x6, other arithmetic, attend(): row_sum = row_sum * factor + exponent.sum(-1)  9.38 us
    squeeze x4, local copies, waits for them, and re-layouts, per_device(): lax.scan(inner_step, state, (portion.reshape(-1, block_rows, portion.shap...  6.93 us
  transfers between devices with their start and end apart: 2, of which 2 were waited for; matrix products, arithmetic and copies ran while one was open for 5% of the time, Pallas kernels for 0%

commit v1 on v0

v1 whole, which is shorter than its diff:
```python
import functools

import jax
import jax.numpy as jnp
import numpy as np
from jax import lax
from jax.experimental import pallas as pl
from jax.experimental.pallas import tpu as pltpu
from jax.sharding import Mesh
from jax.sharding import PartitionSpec as P

HD = 128
ROWS = 128
KVH = 8
GROUP = 4
CACHE = 256
N_CTX = 32
DOCS = 8
QW = GROUP * HD
MIB = 1024 * 1024

CTX = ("x", "h", "l", "c")


def hadamard(length):
    numbers = np.arange(length)
    common = numbers[:, None] & numbers[None, :]
    parity = np.zeros((length, length), np.int64)
    for bit_place in range(max(int(length).bit_length(), 1)):
        parity = parity ^ common >> bit_place & 1
    return 1.0 - 2.0 * parity


def dot(a, b, dims):
    return lax.dot_general(a, b, (dims, ((), ())), preferred_element_type=jnp.float32)


def pack_q_kernel(q_ref, o_ref):
    for i in range(o_ref.shape[0]):
        o_ref[i] = q_ref[:, i * QW : (i + 1) * QW]


def pack_q(queries):
    steps = 2
    per = KVH // steps
    return pl.pallas_call(
        pack_q_kernel,
        grid=(steps,),
        in_specs=[pl.BlockSpec((ROWS, per * QW), lambda i: (0, i))],
        out_specs=pl.BlockSpec((per, ROWS, QW), lambda i: (i, 0, 0)),
        out_shape=jax.ShapeDtypeStruct((KVH, ROWS, QW), jnp.bfloat16),
        cost_estimate=pl.CostEstimate(flops=0, bytes_accessed=4 * KVH * ROWS * QW, transcendentals=0),
        compiler_params=pltpu.CompilerParams(vmem_limit_bytes=60 * MIB),
        name="pack_q",
    )(queries)


def pack_kv_kernel(k_ref, v_ref, o_ref):
    for i in range(o_ref.shape[0]):
        for low in range(2):
            lanes = slice((2 * i + low) * HD, (2 * i + low + 1) * HD)
            keys = k_ref[:, lanes]
            values = v_ref[:, lanes].T
            for high in range(2):
                o_ref[i, high, low, 0] = keys
                o_ref[i, high, low, 1] = values


def pack_kv(keys, values):
    steps = 2
    per = 4 // steps
    return pl.pallas_call(
        pack_kv_kernel,
        grid=(steps,),
        in_specs=[pl.BlockSpec((ROWS, 2 * per * HD), lambda i: (0, i))] * 2,
        out_specs=pl.BlockSpec((per, 2, 2, 2, ROWS, HD), lambda i: (i, 0, 0, 0, 0, 0)),
        out_shape=jax.ShapeDtypeStruct((4, 2, 2, 2, ROWS, HD), jnp.bfloat16),
        cost_estimate=pl.CostEstimate(flops=0, bytes_accessed=6 * KVH * ROWS * QW // 2, transcendentals=0),
        compiler_params=pltpu.CompilerParams(vmem_limit_bytes=60 * MIB),
        name="pack_kv",
    )(keys, values)


def turn_kernel(place, ck_ref, cv_ref, had_ref, sk_ref, sv_ref, k_out, v_out):
    had = had_ref[...]
    for d in range(k_out.shape[0]):
        rows = slice(d * CACHE, (d + 1) * CACHE)
        turned = dot(ck_ref[0, rows, :], had, ((1,), (0,))) * np.float32(HD**-0.5)
        k_out[d] = (turned * sk_ref[...]).astype(jnp.bfloat16)
        turned = dot(had, cv_ref[0, rows, :], ((1,), (1,))) * np.float32(HD**-0.5)
        v_out[d] = (turned * sv_ref[...]).astype(jnp.bfloat16)


def turn_cache(place, cache, had, sign_k, sign_v):
    whole = pl.BlockSpec(memory_space=pltpu.VMEM)
    rows = DOCS * CACHE
    return pl.pallas_call(
        turn_kernel,
        grid_spec=pltpu.PrefetchScalarGridSpec(
            num_scalar_prefetch=1,
            grid=(1,),
            in_specs=[
                pl.BlockSpec((1, rows, HD), lambda i, at: (0, 0, at[0] * 2 + at[2])),
                pl.BlockSpec((1, rows, HD), lambda i, at: (0, 0, KVH + at[0] * 2 + at[2])),
                pl.BlockSpec((HD, HD), lambda i, at: (0, 0)),
                pl.BlockSpec((1, HD), lambda i, at: (0, 0)),
                pl.BlockSpec((HD, 1), lambda i, at: (0, 0)),
            ],
            out_specs=[whole, whole],
        ),
        out_shape=[
            jax.ShapeDtypeStruct((DOCS, CACHE, HD), jnp.bfloat16),
            jax.ShapeDtypeStruct((DOCS, HD, CACHE), jnp.bfloat16),
        ],
        cost_estimate=pl.CostEstimate(flops=8 * DOCS * CACHE * HD * HD, bytes_accessed=8 * DOCS * CACHE * HD, transcendentals=0),
        compiler_params=pltpu.CompilerParams(vmem_limit_bytes=56 * MIB),
        name="turn_cache",
    )(place, cache, cache, had, sign_k, sign_v)


PAIR = 2 * ROWS
MOST_PAIRS = 8
SIZES = (4, 2, 1)
BOTH = range(2)


def attend_kernel(
    begin,
    place,
    docs,
    firsts,
    q_ref,
    k_ref,
    v_ref,
    ck_hbm,
    cv_hbm,
    o_ref,
    ck_ref,
    cv_ref,
    sem,
    qt,
    scores,
    acc,
    tops,
    sums,
):
    src_x = lax.rem(place[0] + begin + 2 * pl.program_id(0), 4)
    scale = np.float32(HD**-0.5 * np.log2(np.e))
    mes = [src_x * 8 + place[1] * 4 + n * 2 + place[3] for n in BOTH]
    first = [firsts[me] for me in mes]
    doc = [docs[me] for me in mes]
    before = [mes[n] - first[n] for n in BOTH]
    pairs = [before[n] // 2 for n in BOTH]
    beside = [jnp.maximum(me - 1, 0) for me in mes]

    k_copy = pltpu.make_async_copy(ck_hbm, ck_ref, sem.at[0])
    v_copy = pltpu.make_async_copy(cv_hbm, cv_ref, sem.at[1])

    @pl.when(pl.program_id(0) == 0)
    def _():
        k_copy.start()
        v_copy.start()

    def fold(s):
        return s.reshape(-1, 8, QW)

    def regions(n, work):
        big = SIZES[0]

        def body(i, carry):
            work(n, i * big, big)
            return carry

        lax.fori_loop(0, pairs[n] // big, body, 0)
        done = pairs[n] // big * big
        for size in SIZES[1:]:
            need = (pairs[n] & size) != 0

            @pl.when(need)
            def _(done=done, size=size):
                work(n, done, size)

            done = done + jnp.where(need, size, 0)

    key_at = lax.broadcasted_iota(jnp.int32, (PAIR, QW), 0)
    query_at = lax.broadcasted_iota(jnp.int32, (PAIR, QW), 1) % ROWS + ROWS
    causal = key_at <= query_at
    for n in BOTH:
        for g in range(GROUP):
            lanes = slice(g * HD, (g + 1) * HD)
            qt[n, :, lanes] = q_ref[n, :, lanes].T
    for n in BOTH:
        keys = jnp.concatenate([k_ref[beside[n]], k_ref[mes[n]]], axis=0)
        lowest = jnp.where(before[n] % 2 == 1, 0, ROWS)
        s_own = dot(keys, qt[n], ((1,), (0,)))
        s_own = jnp.where(causal & (key_at >= lowest), s_own, -jnp.inf)
        scores[n, 1] = s_own
        tops[n] = jnp.max(fold(s_own), axis=0)

    def look(n, begin_at, count):
        best = tops[n]
        for j in range(count):
            i = begin_at + j
            keys = k_ref[pl.ds(first[n] + 2 * i, 2)].reshape(PAIR, HD)
            s = dot(keys, qt[n], ((1,), (0,)))
            scores[n, 2 + i] = s
            best = jnp.maximum(best, jnp.max(fold(s), axis=0))
        tops[n] = best

    for n in BOTH:
        regions(n, look)

    @pl.when(pl.program_id(0) == 0)
    def _():
        k_copy.wait()
        v_copy.wait()

    for n in BOTH:
        s_cache = dot(ck_ref[doc[n]], qt[n], ((1,), (0,)))
        scores[n, 0] = s_cache
        top = jnp.maximum(tops[n], jnp.max(fold(s_cache), axis=0))
        tops[n] = jnp.broadcast_to(jnp.max(top, axis=0, keepdims=True) * scale, (8, QW))

    def weigh(n, i, top):
        p = jnp.exp2(scores[n, i] * scale - top)
        return p.astype(jnp.bfloat16), jnp.sum(fold(p), axis=0)

    for n in BOTH:
        top = tops[n, 0:1]
        p_cache, l_cache = weigh(n, 0, top)
        p_own, l_own = weigh(n, 1, top)
        values = jnp.concatenate([v_ref[beside[n]], v_ref[mes[n]]], axis=1)
        acc[n] = dot(cv_ref[doc[n]], p_cache, ((1,), (0,))) + dot(values, p_own, ((1,), (0,)))
        sums[n] = l_cache + l_own

    def add(n, begin_at, count):
        top = tops[n, 0:1]
        total = sums[n]
        out = acc[n]
        for j in range(count):
            i = begin_at + j
            p, l = weigh(n, 2 + i, top)
            at = first[n] + 2 * i
            values = jnp.concatenate([v_ref[at], v_ref[at + 1]], axis=1)
            out = out + dot(values, p, ((1,), (0,)))
            total = total + l
        sums[n] = total
        acc[n] = out

    for n in BOTH:
        regions(n, add)

    for n in BOTH:
        out = acc[n] * (1.0 / jnp.sum(sums[n], axis=0, keepdims=True))
        for g in range(GROUP):
            lanes = slice(g * HD, (g + 1) * HD)
            o_ref[n, :, lanes] = out[:, lanes].astype(jnp.bfloat16).T


def attend(begin, steps, place, docs, firsts, queries, keys, values, cache_k, cache_v):
    def q_at(i, place, docs, firsts):
        return (lax.rem(place[0] + begin + 2 * i, 4), 0, 0)

    whole = pl.BlockSpec(memory_space=pltpu.VMEM)
    there = pl.BlockSpec(memory_space=pl.ANY)
    return pl.pallas_call(
        functools.partial(attend_kernel, begin),
        grid_spec=pltpu.PrefetchScalarGridSpec(
            num_scalar_prefetch=3,
            grid=(steps,),
            in_specs=[pl.BlockSpec((2, ROWS, QW), q_at), whole, whole, there, there],
            out_specs=pl.BlockSpec((2, ROWS, QW), lambda i, place, docs, firsts: (i, 0, 0)),
            scratch_shapes=[
                pltpu.VMEM((DOCS, CACHE, HD), jnp.bfloat16),
                pltpu.VMEM((DOCS, HD, CACHE), jnp.bfloat16),
                pltpu.SemaphoreType.DMA((2,)),
                pltpu.VMEM((2, HD, QW), jnp.bfloat16),
                pltpu.VMEM((2, 2 + MOST_PAIRS, PAIR, QW), jnp.float32),
                pltpu.VMEM((2, HD, QW), jnp.float32),
                pltpu.VMEM((2, 8, QW), jnp.float32),
                pltpu.VMEM((2, 8, QW), jnp.float32),
            ],
        ),
        out_shape=jax.ShapeDtypeStruct((2 * steps, ROWS, QW), jnp.bfloat16),
        compiler_params=pltpu.CompilerParams(vmem_limit_bytes=20 * MIB),
        cost_estimate=pl.CostEstimate(flops=steps * 48 * PAIR * QW * HD, bytes_accessed=steps * 4 * ROWS * QW, transcendentals=steps * 12 * PAIR * QW),
        name="attend",
    )(place, docs, firsts, queries, keys, values, cache_k, cache_v)


def join_kernel(offsets, place, *refs):
    pieces, out, sem = refs[: len(offsets)], refs[-2], refs[-1]
    copies = []
    for i, (dx, dl) in enumerate(offsets):
        head = lax.rem(place[0] + 4 - dx, 4) * 2 + lax.rem(place[2] + dl, 2)
        lanes = pl.ds(pl.multiple_of(head * QW, QW), QW)
        copies.append(pltpu.make_async_copy(pieces[i].at[0], out.at[:, lanes], sem.at[i]))
    for copy in copies:
        copy.start()
    for copy in copies:
        copy.wait()


def join(place, offsets, pieces, base):
    whole = pl.BlockSpec(memory_space=pltpu.VMEM)
    there = pl.BlockSpec(memory_space=pl.ANY)
    known = [] if base is None else [base]
    return pl.pallas_call(
        functools.partial(join_kernel, offsets),
        grid_spec=pltpu.PrefetchScalarGridSpec(
            num_scalar_prefetch=1,
            grid=(1,),
            in_specs=[whole] * len(pieces) + [there] * len(known),
            out_specs=there,
            scratch_shapes=[pltpu.SemaphoreType.DMA((len(pieces),))],
        ),
        out_shape=jax.ShapeDtypeStruct((ROWS, KVH * QW), jnp.bfloat16),
        input_output_aliases={} if base is None else {1 + len(pieces): 0},
        compiler_params=pltpu.CompilerParams(vmem_limit_bytes=4 * MIB),
        name="join",
    )(place, *pieces, *known)


def out_route(sections, dx, dl):
    route = []
    for z in range(sections):
        for x in range(4):
            for l in range(2):
                target = ((z + 1) % sections, (x + dx) % 4, l ^ dl)
                route.append(((z * 4 + x) * 2 + l, (target[0] * 4 + target[1]) * 2 + target[2]))
    return route


def per_device(queries, keys_new, values_new, stretch_cache, hadamard_signs, stretch_docs):
    place = jnp.stack([lax.axis_index(name) for name in CTX]).astype(jnp.int32)
    sections = lax.axis_size("section")
    had = jnp.asarray(hadamard(HD), dtype=jnp.bfloat16)
    signs = hadamard_signs[0].astype(jnp.float32)
    kv = pack_kv(keys_new[0], values_new[0])
    q = pack_q(queries[0])
    mine = lax.all_to_all(kv.reshape(N_CTX, ROWS, HD), CTX, 0, 0, tiled=True)
    cache_k, cache_v = turn_cache(place, stretch_cache, had, signs[0:1], signs[1].reshape(HD, 1))
    earlier = stretch_docs[None, :] < stretch_docs[:, None]
    firsts = jnp.sum(earlier, axis=1, dtype=jnp.int32)
    mine, q, cache_k, cache_v = lax.optimization_barrier((mine, q, cache_k, cache_v))
    other = lax.ppermute(mine, "c", [(0, 1), (1, 0)])
    q = lax.all_to_all(q, ("x", "l"), 0, 0, tiled=True)
    keys = jnp.where(place[3] == 0, mine, other)
    values = jnp.where(place[3] == 0, other, mine)
    result = None
    for begin in range(2):
        out = attend(begin, 2, place, stretch_docs, firsts, q, keys, values, cache_k, cache_v)
        offsets = [(begin + 2 * i, dl) for i in range(2) for dl in range(2)]
        pieces = []
        for i, (dx, dl) in enumerate(offsets):
            row = i // 2 * 2 + (place[2] + dl) % 2
            piece = lax.dynamic_slice_in_dim(out, row, 1, 0)
            pieces.append(lax.ppermute(piece, ("section", "x", "l"), out_route(sections, dx, dl)))
        result = join(place, offsets, pieces, result)
    return result[None]


def solution(mesh):
    sections = mesh.shape["section"]
    split = Mesh(mesh.devices.reshape(sections, 4, 2, 2, 2), ("section",) + CTX)
    rows = P("section", CTX, None)
    in_specs = (rows, rows, rows, P("section", None, None), P("section", None, None), P())
    return jax.shard_map(
        per_device, mesh=split, in_specs=in_specs, out_specs=rows, check_vma=False
    )
```

time: 227 us -> 90.6 us (0.40)
  waiting for transfers between devices: 92 us -> 27.5 us
  local copies, waits for them, and re-layouts: 44.7 us -> 3.5 us
  other arithmetic: 39 us -> 3.15 us
  starting transfers between devices: 1.63 us -> 32.3 us
  matrix products: 27.1 us -> 0 us
  Pallas kernels: 0 us -> 22.8 us
  between operations: 14.3 us -> 0.27 us
  loops' own time: 5.57 us -> 0 us
    all_gather x1 -> x0, waiting for transfers between devices: 66.6 us -> none  [per_device(): portion = lax.all_gather(new_front, 'ctx', axis=0, tiled=True)]
    dot_general x16 -> x0, matrix products: 27.1 us -> none  [the longest x6 14.2 us: attend(): jnp.einsum('rkgn,nkd->rkgd', exponent.astype(jnp.bfloat16), value_part, p...]
    pallas_call x0 -> x7, Pallas kernels: none -> 22.8 us  [the longest x2 12.5 us: attend(): pl.pallas_call(functools.partial(attend_kernel, begin), grid_spec=pltpu.P...]
    unnamed x13 -> x10, local copies, waits for them, and re-layouts: 24.6 us -> 2.09 us
    all_to_all x0 -> x2, waiting for transfers between devices: none -> 20.6 us  [the longest x1 14.2 us: per_device(): q = lax.all_to_all(q, ('x', 'l'), 0, 0, tiled=True)]
    ppermute x1 -> x9, starting transfers between devices: 1.63 us -> 20.2 us  [the longest x8 19.8 us: per_device(): lax.ppermute(piece, ('section', 'x', 'l'), out_route(sections, dx, dl))]
    ppermute x1 -> x9, waiting for transfers between devices: 25.3 us -> 6.89 us  [the longest x8 6.89 us: per_device(): lax.ppermute(piece, ('section', 'x', 'l'), out_route(sections, dx, dl))]
    reduce_or x8 -> x0, other arithmetic: 15.4 us -> none  [attend_columns(): jnp.any(allowed)]
  transfers between devices with their start and end apart: 2 -> 11, of which waited for: 2 -> 5; matrix products, arithmetic and copies ran while one was open for 5% -> 5% of each run, Pallas kernels for 0% -> 15%
where the time goes in v1:
time: 90.6 us; the launch traced here: 89.4 us
  starting transfers between devices  32.3 us (36%)
  waiting for transfers between devices  27.5 us (30%)
  Pallas kernels  22.8 us (25%)
  local copies, waits for them, and re-layouts  3.5 us (4%)
  other arithmetic  3.15 us (3%)
    ppermute x8, starting transfers between devices, per_device(): lax.ppermute(piece, ('section', 'x', 'l'), out_route(sections, dx, dl))  19.8 us
    all_to_all x1, waiting for transfers between devices, per_device(): q = lax.all_to_all(q, ('x', 'l'), 0, 0, tiled=True)  14.2 us
    pallas_call x2, Pallas kernels, attend(): pl.pallas_call(functools.partial(attend_kernel, begin), grid_spec=pltpu.P...  12.5 us
    all_to_all x1, starting transfers between devices, per_device(): mine = lax.all_to_all(kv.reshape(N_CTX, ROWS, HD), CTX, 0, 0, tiled=True)  7.28 us
    ppermute x8, waiting for transfers between devices, per_device(): lax.ppermute(piece, ('section', 'x', 'l'), out_route(sections, dx, dl))  6.89 us
    all_to_all x1, waiting for transfers between devices, per_device(): mine = lax.all_to_all(kv.reshape(N_CTX, ROWS, HD), CTX, 0, 0, tiled=True)  6.41 us
    all_to_all x1, starting transfers between devices, per_device(): q = lax.all_to_all(q, ('x', 'l'), 0, 0, tiled=True)  4.82 us
    pallas_call x1, Pallas kernels, turn_cache(): pl.pallas_call(turn_kernel, grid_spec=pltpu.PrefetchScalarGridSpec(num_sc...  3.41 us
  transfers between devices with their start and end apart: 11, of which 5 were waited for; matrix products, arithmetic and copies ran while one was open for 5% of the time, Pallas kernels for 15%

profile of v1, /device:TPU:26, one launch (start us, length us, event | category | flops | bytes accessed | tf_op | source)
XLA Modules:
  0.0 89.4 jit_solution(758389661983244083)
XLA Ops:
  0.0 2.1 %pack_kv.1 = bf16[4,2,2,2,128,128]{5,4,3,2,1,0:T(8,128)(2,1)} custom-call(bf16[128,1024]{1,0:T(8,128)(2,1)} %bitcast.15, bf16[128,1024]{1,0:T(8,128)(2,1)} %bitcast.16), custom_call_target="tpu_custom_call" | custom-call | bytes 1572864 | tf_op jit(solution)/shard_map/pack_kv/pallas_call | solution.py:72
  2.1 7.3 %all-to-all-start = ((bf16[32,128,128]{2,1,0:T(8,128)(2,1)}), bf16[32,128,128]{2,1,0:T(8,128)(2,1)S(1)}, u32[]{:S(2)}, u32[]{:S(2)}) async-start(bf16[32,128,128]{2,1,0:T(8,128)(2,1)} %bitcast.13), calls=%async_computation | async-start | bytes 2097152 | tf_op jit(solution)/shard_map/all_to_all | solution.py:341
  9.4 0.7 convert_element_type.8
  10.0 0.6 slice_bitcast_fusion
  10.6 0.7 copy.10.sv_ref
  11.4 2.0 %pack_q.1 = bf16[8,128,512]{2,1,0:T(8,128)(2,1)} custom-call(bf16[128,4096]{1,0:T(8,128)(2,1)} %bitcast.14), custom_call_target="tpu_custom_call" | custom-call | bytes 2097152 | tf_op jit(solution)/shard_map/pack_q/pallas_call | solution.py:46
  13.4 0.6 pad_add_fusion.place
  14.0 3.4 %turn_cache.1 = (bf16[8,256,128]{2,1,0:T(8,128)(2,1)}, bf16[8,128,256]{2,1,0:T(8,128)(2,1)}) custom-call(s32[4]{0:T(128)} %pad_add_fusion.place, bf16[1,2048,2048]{2,1,0:T(8,128)(2,1)} %cv_ref.1, bf16[1,2048,2048]{2,1,0:T(8,128)(2,1)} %cv_ref.1, bf16[128,128]{1,0:T(8,128)(2,1)} %constant.52.clone.had_ref, f32[1,128]{1,0:T(1,128)} %get-tuple-element.28.sk_ref, ...), custom_call_target="tpu_custom_call" | custom-call | flops 268435456 | bytes 2097152 | tf_op jit(solution)/shard_map/turn_cache/pallas_call | solution.py:97
  17.4 6.4 %all-to-all-done = bf16[32,128,128]{2,1,0:T(8,128)(2,1)S(1)} async-done(((bf16[32,128,128]{2,1,0:T(8,128)(2,1)}), bf16[32,128,128]{2,1,0:T(8,128)(2,1)S(1)}, u32[]{:S(2)}, u32[]{:S(2)}) %all-to-all-start) | async-done | bytes 1048608 | tf_op jit(solution)/shard_map/all_to_all | solution.py:341
  23.8 0.3 collective-permute-start
  24.2 4.8 %all-to-all-start.1 = ((bf16[8,128,512]{2,1,0:T(8,128)(2,1)}), bf16[8,128,512]{2,1,0:T(8,128)(2,1)S(1)}, u32[]{:S(2)}, u32[]{:S(2)}) async-start(bf16[8,128,512]{2,1,0:T(8,128)(2,1)} %pack_q.1), calls=%async_computation.1 | async-start | bytes 2097152 | tf_op jit(solution)/shard_map/all_to_all | solution.py:347
  29.0 0.2 convert_reduce_fusion.firsts
  29.2 0.0 collective-permute-done
  29.2 1.7 %broadcast_select_fusion = (bf16[32,128,128]{2,1,0:T(8,128)(2,1)S(1)}, bf16[32,128,128]{2,1,0:T(8,128)(2,1)S(1)}) fusion(bf16[32,128,128]{2,1,0:T(8,128)(2,1)} %collective-permute-done, bf16[32,128,128]{2,1,0:T(8,128)(2,1)} %copy-done.4, pred[]{:T(512)S(6)} %eq.13), kind=kLoop, calls=%fused_computation | loop fusion | flops 1048576 | bytes 4194305 | tf_op jit(solution)/shard_map/jit(_where)/select_n | solution.py:349
  30.9 14.2 %all-to-all-done.1.q_ref = bf16[8,128,512]{2,1,0:T(8,128)(2,1)S(1)} async-done(((bf16[8,128,512]{2,1,0:T(8,128)(2,1)}), bf16[8,128,512]{2,1,0:T(8,128)(2,1)S(1)}, u32[]{:S(2)}, u32[]{:S(2)}) %all-to-all-start.1) | async-done | bytes 1048608 | tf_op jit(solution)/shard_map/all_to_all | solution.py:347
  45.1 1.0 %copy-done.1 = bf16[8,256,128]{2,1,0:T(8,128)(2,1)S(1)} copy-done((bf16[8,256,128]{2,1,0:T(8,128)(2,1)S(1)}, bf16[8,256,128]{2,1,0:T(8,128)(2,1)}, u32[]{:S(2)}) %copy-start.1) | copy-done | bytes 524312
  46.1 1.0 %copy-done.2 = bf16[8,128,256]{2,1,0:T(8,128)(2,1)S(1)} copy-done((bf16[8,128,256]{2,1,0:T(8,128)(2,1)S(1)}, bf16[8,128,256]{2,1,0:T(8,128)(2,1)}, u32[]{:S(2)}) %copy-start.2) | copy-done | bytes 524312
  47.1 5.5 %attend.3 = bf16[4,128,512]{2,1,0:T(8,128)(2,1)S(1)} custom-call(s32[4]{0:T(128)S(1)} %copy-done, s32[32]{0:T(128)S(1)} %copy-done.3, s32[32]{0:T(128)S(1)} %convert_reduce_fusion.firsts, bf16[8,128,512]{2,1,0:T(8,128)(2,1)S(1)} %all-to-all-done.1.q_ref, bf16[32,128,128]{2,1,0:T(8,128)(2,1)S(1)} %get-tuple-element.18.k_ref, ...), custom_call_target="tpu_custom_call" | custom-call | flops 1610612736 | bytes 524288 | tf_op jit(solution)/shard_map/attend/pallas_call | solution.py:266
  52.7 2.0 %collective-permute-start.5 = (bf16[1,128,512]{2,1,0:T(8,128)(2,1)S(1)}, bf16[1,128,512]{2,1,0:T(8,128)(2,1)S(1)}, u32[]{:S(2)}, u32[]{:S(2)}) collective-permute-start(bf16[1,128,512]{2,1,0:T(8,128)(2,1)S(1)} %get-tuple-element.22), channel_id=1, source_target_pairs={{0,32},{2,34},{8,40},{10,42},{16,48},{18,50},{24,56},{26,58},{32,6... | collective-permute-start | bytes 393224 | tf_op jit(solution)/shard_map/ppermute | solution.py:358
  54.7 2.0 %collective-permute-start.6 = (bf16[1,128,512]{2,1,0:T(8,128)(2,1)S(1)}, bf16[1,128,512]{2,1,0:T(8,128)(2,1)S(1)}, u32[]{:S(2)}, u32[]{:S(2)}) collective-permute-start(bf16[1,128,512]{2,1,0:T(8,128)(2,1)S(1)} %get-tuple-element.21), channel_id=1, source_target_pairs={{0,34},{2,32},{8,42},{10,40},{16,50},{18,48},{24,58},{26,56},{32,6... | collective-permute-start | bytes 393224 | tf_op jit(solution)/shard_map/ppermute | solution.py:358
  56.7 1.6 %collective-permute-start.7 = (bf16[1,128,512]{2,1,0:T(8,128)(2,1)S(1)}, bf16[1,128,512]{2,1,0:T(8,128)(2,1)S(1)}, u32[]{:S(2)}, u32[]{:S(2)}) collective-permute-start(bf16[1,128,512]{2,1,0:T(8,128)(2,1)S(1)} %get-tuple-element.20), channel_id=1, source_target_pairs={{0,48},{2,50},{8,56},{10,58},{16,32},{18,34},{24,40},{26,42},{32,8... | collective-permute-start | bytes 393224 | tf_op jit(solution)/shard_map/ppermute | solution.py:358
  58.3 6.7 %collective-permute-start.8 = (bf16[1,128,512]{2,1,0:T(8,128)(2,1)S(1)}, bf16[1,128,512]{2,1,0:T(8,128)(2,1)S(1)}, u32[]{:S(2)}, u32[]{:S(2)}) collective-permute-start(bf16[1,128,512]{2,1,0:T(8,128)(2,1)S(1)} %get-tuple-element.19), channel_id=1, source_target_pairs={{0,50},{2,48},{8,58},{10,56},{16,34},{18,32},{24,42},{26,40},{32,8... | collective-permute-start | bytes 393224 | tf_op jit(solution)/shard_map/ppermute | solution.py:358
  65.0 7.0 %attend.2 = bf16[4,128,512]{2,1,0:T(8,128)(2,1)S(1)} custom-call(s32[4]{0:T(128)S(1)} %copy-done, s32[32]{0:T(128)S(1)} %copy-done.3, s32[32]{0:T(128)S(1)} %convert_reduce_fusion.firsts, bf16[8,128,512]{2,1,0:T(8,128)(2,1)S(1)} %all-to-all-done.1.q_ref, bf16[32,128,128]{2,1,0:T(8,128)(2,1)S(1)} %get-tuple-element.18.k_ref, ...), custom_call_target="tpu_custom_call" | custom-call | flops 1610612736 | bytes 524288 | tf_op jit(solution)/shard_map/attend/pallas_call | solution.py:266
  72.0 0.1 collective-permute-start.1
  72.1 1.7 %collective-permute-start.2 = (bf16[1,128,512]{2,1,0:T(8,128)(2,1)S(1)}, bf16[1,128,512]{2,1,0:T(8,128)(2,1)S(1)}, u32[]{:S(2)}, u32[]{:S(2)}) collective-permute-start(bf16[1,128,512]{2,1,0:T(8,128)(2,1)S(1)} %get-tuple-element.25), channel_id=1, source_target_pairs={{0,42},{2,40},{8,50},{10,48},{16,58},{18,56},{24,34},{26,32},{32,7... | collective-permute-start | bytes 393224 | tf_op jit(solution)/shard_map/ppermute | solution.py:358
  73.9 1.8 %collective-permute-start.3 = (bf16[1,128,512]{2,1,0:T(8,128)(2,1)S(1)}, bf16[1,128,512]{2,1,0:T(8,128)(2,1)S(1)}, u32[]{:S(2)}, u32[]{:S(2)}) collective-permute-start(bf16[1,128,512]{2,1,0:T(8,128)(2,1)S(1)} %get-tuple-element.24), channel_id=1, source_target_pairs={{0,56},{2,58},{8,32},{10,34},{16,40},{18,42},{24,48},{26,50},{32,8... | collective-permute-start | bytes 393224 | tf_op jit(solution)/shard_map/ppermute | solution.py:358
  75.7 4.0 %collective-permute-start.4 = (bf16[1,128,512]{2,1,0:T(8,128)(2,1)S(1)}, bf16[1,128,512]{2,1,0:T(8,128)(2,1)S(1)}, u32[]{:S(2)}, u32[]{:S(2)}) collective-permute-start(bf16[1,128,512]{2,1,0:T(8,128)(2,1)S(1)} %get-tuple-element.23), channel_id=1, source_target_pairs={{0,58},{2,56},{8,34},{10,32},{16,42},{18,40},{24,50},{26,48},{32,9... | collective-permute-start | bytes 393224 | tf_op jit(solution)/shard_map/ppermute | solution.py:358
  79.6 1.4 %join.2.refs_4_ = bf16[128,4096]{1,0:T(8,128)(2,1)} custom-call(s32[4]{0:T(128)S(1)} %copy-done, bf16[1,128,512]{2,1,0:T(8,128)(2,1)S(1)} %collective-permute-done.5.refs_0_, bf16[1,128,512]{2,1,0:T(8,128)(2,1)S(1)} %collective-permute-done.6.refs_1_, bf16[1,128,512]{2,1,0:T(8,128)(2,1)S(1)} %collective-permute-done.7.refs_2_, ...), custom_call_target="tpu_custom_call" | custom-call | tf_op jit(solution)/shard_map/join/pallas_call | solution.py:308
  81.0 1.6 %collective-permute-done.2.refs_1_ = bf16[1,128,512]{2,1,0:T(8,128)(2,1)S(1)} collective-permute-done((bf16[1,128,512]{2,1,0:T(8,128)(2,1)S(1)}, bf16[1,128,512]{2,1,0:T(8,128)(2,1)S(1)}, u32[]{:S(2)}, u32[]{:S(2)}) %collective-permute-start.2) | collective-permute-done | bytes 131104 | tf_op jit(solution)/shard_map/ppermute | solution.py:358
  82.7 3.1 %collective-permute-done.3.refs_2_ = bf16[1,128,512]{2,1,0:T(8,128)(2,1)S(1)} collective-permute-done((bf16[1,128,512]{2,1,0:T(8,128)(2,1)S(1)}, bf16[1,128,512]{2,1,0:T(8,128)(2,1)S(1)}, u32[]{:S(2)}, u32[]{:S(2)}) %collective-permute-start.3) | collective-permute-done | bytes 131104 | tf_op jit(solution)/shard_map/ppermute | solution.py:358
  85.8 2.2 %collective-permute-done.4.refs_3_ = bf16[1,128,512]{2,1,0:T(8,128)(2,1)S(1)} collective-permute-done((bf16[1,128,512]{2,1,0:T(8,128)(2,1)S(1)}, bf16[1,128,512]{2,1,0:T(8,128)(2,1)S(1)}, u32[]{:S(2)}, u32[]{:S(2)}) %collective-permute-start.4) | collective-permute-done | bytes 131104 | tf_op jit(solution)/shard_map/ppermute | solution.py:358
  87.9 1.4 %join.3 = bf16[128,4096]{1,0:T(8,128)(2,1)} custom-call(s32[4]{0:T(128)S(1)} %copy-done, bf16[1,128,512]{2,1,0:T(8,128)(2,1)S(1)} %collective-permute-done.1.refs_0_, bf16[1,128,512]{2,1,0:T(8,128)(2,1)S(1)} %collective-permute-done.2.refs_1_, bf16[1,128,512]{2,1,0:T(8,128)(2,1)S(1)} %collective-permute-done.3.refs_2_, ...), custom_call_target="tpu_custom_call", output_to_operand_aliasing={{}: (5, {})} | custom-call | tf_op jit(solution)/shard_map/join/pallas_call | solution.py:308
  (15 shorter events, 0.1 us)
Async XLA Ops:
  2.1 21.8 %all-to-all-start = ((bf16[32,128,128]{2,1,0:T(8,128)(2,1)}), bf16[32,128,128]{2,1,0:T(8,128)(2,1)S(1)}, u32[]{:S(2)}, u32[]{:S(2)}) async-start(bf16[32,128,128]{2,1,0:T(8,128)(2,1)} %bitcast.13), calls=%async_computation | async-start | bytes 2097152 | tf_op jit(solution)/shard_map/all_to_all | solution.py:341
  14.0 15.0 %copy-start.3 = (s32[32]{0:T(128)S(1)}, s32[32]{0:T(128)}, u32[]{:S(2)}) copy-start(s32[32]{0:T(128)} %docs.3) | copy-start | bytes 388
  14.0 31.1 %copy-start = (s32[4]{0:T(128)S(1)}, s32[4]{0:T(128)}, u32[]{:S(2)}) copy-start(s32[4]{0:T(128)} %pad_add_fusion.place) | copy-start | bytes 52
  23.8 5.4 %copy-start.4 = (bf16[32,128,128]{2,1,0:T(8,128)(2,1)}, bf16[32,128,128]{2,1,0:T(8,128)(2,1)S(1)}, u32[]{:S(2)}) copy-start(bf16[32,128,128]{2,1,0:T(8,128)(2,1)S(1)} %all-to-all-done) | copy-start | bytes 3145732
  23.8 5.4 %collective-permute-start = (bf16[32,128,128]{2,1,0:T(8,128)(2,1)S(1)}, bf16[32,128,128]{2,1,0:T(8,128)(2,1)}, u32[]{:S(2)}, u32[]{:S(2)}) collective-permute-start(bf16[32,128,128]{2,1,0:T(8,128)(2,1)S(1)} %all-to-all-done), channel_id=1, source_target_pairs={{0,1},{1,0},{2,3},{3,2},{4,5},{5,4},{6,7},{7,6},{8,9},{9,8},{10,11... | collective-permute-start | bytes 3145736 | tf_op jit(solution)/shard_map/ppermute | solution.py:346
  24.2 20.9 %all-to-all-start.1 = ((bf16[8,128,512]{2,1,0:T(8,128)(2,1)}), bf16[8,128,512]{2,1,0:T(8,128)(2,1)S(1)}, u32[]{:S(2)}, u32[]{:S(2)}) async-start(bf16[8,128,512]{2,1,0:T(8,128)(2,1)} %pack_q.1), calls=%async_computation.1 | async-start | bytes 2097152 | tf_op jit(solution)/shard_map/all_to_all | solution.py:347
  45.1 1.0 %copy-start.1 = (bf16[8,256,128]{2,1,0:T(8,128)(2,1)S(1)}, bf16[8,256,128]{2,1,0:T(8,128)(2,1)}, u32[]{:S(2)}) copy-start(bf16[8,256,128]{2,1,0:T(8,128)(2,1)} %get-tuple-element.15.ck_hbm) | copy-start | bytes 1572868
  46.1 1.0 %copy-start.2 = (bf16[8,128,256]{2,1,0:T(8,128)(2,1)S(1)}, bf16[8,128,256]{2,1,0:T(8,128)(2,1)}, u32[]{:S(2)}) copy-start(bf16[8,128,256]{2,1,0:T(8,128)(2,1)} %get-tuple-element.16.cv_hbm) | copy-start | bytes 1572868
  52.7 19.4 %collective-permute-start.5 = (bf16[1,128,512]{2,1,0:T(8,128)(2,1)S(1)}, bf16[1,128,512]{2,1,0:T(8,128)(2,1)S(1)}, u32[]{:S(2)}, u32[]{:S(2)}) collective-permute-start(bf16[1,128,512]{2,1,0:T(8,128)(2,1)S(1)} %get-tuple-element.22), channel_id=1, source_target_pairs={{0,32},{2,34},{8,40},{10,42},{16,48},{18,50},{24,56},{26,58},{32,6... | collective-permute-start | bytes 393224 | tf_op jit(solution)/shard_map/ppermute | solution.py:358
  54.7 19.2 %collective-permute-start.6 = (bf16[1,128,512]{2,1,0:T(8,128)(2,1)S(1)}, bf16[1,128,512]{2,1,0:T(8,128)(2,1)S(1)}, u32[]{:S(2)}, u32[]{:S(2)}) collective-permute-start(bf16[1,128,512]{2,1,0:T(8,128)(2,1)S(1)} %get-tuple-element.21), channel_id=1, source_target_pairs={{0,34},{2,32},{8,42},{10,40},{16,50},{18,48},{24,58},{26,56},{32,6... | collective-permute-start | bytes 393224 | tf_op jit(solution)/shard_map/ppermute | solution.py:358
  56.7 19.0 %collective-permute-start.7 = (bf16[1,128,512]{2,1,0:T(8,128)(2,1)S(1)}, bf16[1,128,512]{2,1,0:T(8,128)(2,1)S(1)}, u32[]{:S(2)}, u32[]{:S(2)}) collective-permute-start(bf16[1,128,512]{2,1,0:T(8,128)(2,1)S(1)} %get-tuple-element.20), channel_id=1, source_target_pairs={{0,48},{2,50},{8,56},{10,58},{16,32},{18,34},{24,40},{26,42},{32,8... | collective-permute-start | bytes 393224 | tf_op jit(solution)/shard_map/ppermute | solution.py:358
  58.3 21.4 %collective-permute-start.8 = (bf16[1,128,512]{2,1,0:T(8,128)(2,1)S(1)}, bf16[1,128,512]{2,1,0:T(8,128)(2,1)S(1)}, u32[]{:S(2)}, u32[]{:S(2)}) collective-permute-start(bf16[1,128,512]{2,1,0:T(8,128)(2,1)S(1)} %get-tuple-element.19), channel_id=1, source_target_pairs={{0,50},{2,48},{8,58},{10,56},{16,34},{18,32},{24,42},{26,40},{32,8... | collective-permute-start | bytes 393224 | tf_op jit(solution)/shard_map/ppermute | solution.py:358
  72.0 9.0 %collective-permute-start.1 = (bf16[1,128,512]{2,1,0:T(8,128)(2,1)S(1)}, bf16[1,128,512]{2,1,0:T(8,128)(2,1)S(1)}, u32[]{:S(2)}, u32[]{:S(2)}) collective-permute-start(bf16[1,128,512]{2,1,0:T(8,128)(2,1)S(1)} %get-tuple-element.26), channel_id=1, source_target_pairs={{0,40},{2,42},{8,48},{10,50},{16,56},{18,58},{24,32},{26,34},{32,7... | collective-permute-start | bytes 393224 | tf_op jit(solution)/shard_map/ppermute | solution.py:358
  72.1 10.5 %collective-permute-start.2 = (bf16[1,128,512]{2,1,0:T(8,128)(2,1)S(1)}, bf16[1,128,512]{2,1,0:T(8,128)(2,1)S(1)}, u32[]{:S(2)}, u32[]{:S(2)}) collective-permute-start(bf16[1,128,512]{2,1,0:T(8,128)(2,1)S(1)} %get-tuple-element.25), channel_id=1, source_target_pairs={{0,42},{2,40},{8,50},{10,48},{16,58},{18,56},{24,34},{26,32},{32,7... | collective-permute-start | bytes 393224 | tf_op jit(solution)/shard_map/ppermute | solution.py:358
  73.9 11.9 %collective-permute-start.3 = (bf16[1,128,512]{2,1,0:T(8,128)(2,1)S(1)}, bf16[1,128,512]{2,1,0:T(8,128)(2,1)S(1)}, u32[]{:S(2)}, u32[]{:S(2)}) collective-permute-start(bf16[1,128,512]{2,1,0:T(8,128)(2,1)S(1)} %get-tuple-element.24), channel_id=1, source_target_pairs={{0,56},{2,58},{8,32},{10,34},{16,40},{18,42},{24,48},{26,50},{32,8... | collective-permute-start | bytes 393224 | tf_op jit(solution)/shard_map/ppermute | solution.py:358
  75.7 12.2 %collective-permute-start.4 = (bf16[1,128,512]{2,1,0:T(8,128)(2,1)S(1)}, bf16[1,128,512]{2,1,0:T(8,128)(2,1)S(1)}, u32[]{:S(2)}, u32[]{:S(2)}) collective-permute-start(bf16[1,128,512]{2,1,0:T(8,128)(2,1)S(1)} %get-tuple-element.23), channel_id=1, source_target_pairs={{0,58},{2,56},{8,34},{10,32},{16,42},{18,40},{24,50},{26,48},{32,9... | collective-permute-start | bytes 393224 | tf_op jit(solution)/shard_map/ppermute | solution.py:358

commit v2 on v1

v2 whole, which is shorter than its diff:
```python
import functools

import jax
import jax.numpy as jnp
import numpy as np
from jax import lax
from jax.experimental import pallas as pl
from jax.experimental.pallas import tpu as pltpu
from jax.sharding import Mesh
from jax.sharding import PartitionSpec as P

HD = 128
ROWS = 128
KVH = 8
GROUP = 4
CACHE = 256
N_CTX = 32
DOCS = 8
QW = GROUP * HD
MIB = 1024 * 1024
EARLY = (2, 1)
LATE = (3,)
GROUPS = ((0,), (2,), (1, 3))

CTX = ("x", "h", "l", "c")


def hadamard(length):
    numbers = np.arange(length)
    common = numbers[:, None] & numbers[None, :]
    parity = np.zeros((length, length), np.int64)
    for bit_place in range(max(int(length).bit_length(), 1)):
        parity = parity ^ common >> bit_place & 1
    return 1.0 - 2.0 * parity


def dot(a, b, dims):
    return lax.dot_general(a, b, (dims, ((), ())), preferred_element_type=jnp.float32)


def offsets():
    return [(dx, dl) for dx in range(4) for dl in range(2)]


def pack_q_kernel(place, q_ref, *outs):
    for (dx, dl), out in zip(offsets(), outs):
        head = lax.rem(place[0] + 4 - dx, 4) * 2 + lax.rem(place[2] + dl, 2)
        q = q_ref[:, pl.ds(pl.multiple_of(head * QW, QW), QW)]
        for g in range(GROUP):
            lanes = slice(g * HD, (g + 1) * HD)
            out[:, lanes] = q[:, lanes].T


def pack_q(place, queries):
    whole = pl.BlockSpec((ROWS, QW), lambda i, place: (0, 0))
    return pl.pallas_call(
        pack_q_kernel,
        grid_spec=pltpu.PrefetchScalarGridSpec(
            num_scalar_prefetch=1,
            grid=(1,),
            in_specs=[pl.BlockSpec((ROWS, KVH * QW), lambda i, place: (0, 0))],
            out_specs=[whole] * KVH,
        ),
        out_shape=[jax.ShapeDtypeStruct((ROWS, QW), jnp.bfloat16)] * KVH,
        cost_estimate=pl.CostEstimate(flops=0, bytes_accessed=4 * KVH * ROWS * QW, transcendentals=0),
        compiler_params=pltpu.CompilerParams(vmem_limit_bytes=60 * MIB),
        name="pack_q",
    )(place, queries)


def pack_kv_kernel(k_ref, v_ref, o_ref):
    for i in range(o_ref.shape[0]):
        for low in range(2):
            lanes = slice((2 * i + low) * HD, (2 * i + low + 1) * HD)
            keys = k_ref[:, lanes]
            values = v_ref[:, lanes].T
            for high in range(2):
                o_ref[i, high, low, 0] = keys
                o_ref[i, high, low, 1] = values


def pack_kv(keys, values):
    steps = 2
    per = 4 // steps
    return pl.pallas_call(
        pack_kv_kernel,
        grid=(steps,),
        in_specs=[pl.BlockSpec((ROWS, 2 * per * HD), lambda i: (0, i))] * 2,
        out_specs=pl.BlockSpec((per, 2, 2, 2, ROWS, HD), lambda i: (i, 0, 0, 0, 0, 0)),
        out_shape=jax.ShapeDtypeStruct((4, 2, 2, 2, ROWS, HD), jnp.bfloat16),
        cost_estimate=pl.CostEstimate(flops=0, bytes_accessed=6 * KVH * ROWS * QW // 2, transcendentals=0),
        compiler_params=pltpu.CompilerParams(vmem_limit_bytes=60 * MIB),
        name="pack_kv",
    )(keys, values)


def turn_kernel(place, ck_ref, cv_ref, had_ref, out):
    had = had_ref[...]
    for d in range(DOCS):
        rows = slice(d * CACHE, (d + 1) * CACHE)
        turned = dot(ck_ref[0, rows, :], had, ((1,), (0,))) * np.float32(HD**-0.5)
        out[d, 0] = turned.astype(jnp.bfloat16)
        turned = dot(had, cv_ref[0, rows, :], ((1,), (1,))) * np.float32(HD**-0.5)
        turned = turned.astype(jnp.bfloat16)
        for half in range(CACHE // HD):
            lanes = slice(half * HD, (half + 1) * HD)
            out[d, 1, lanes, :] = turned[:, lanes]


def turn_cache(place, cache, had):
    rows = DOCS * CACHE
    return pl.pallas_call(
        turn_kernel,
        grid_spec=pltpu.PrefetchScalarGridSpec(
            num_scalar_prefetch=1,
            grid=(1,),
            in_specs=[
                pl.BlockSpec((1, rows, HD), lambda i, at: (0, 0, at[0] * 2 + at[2])),
                pl.BlockSpec((1, rows, HD), lambda i, at: (0, 0, KVH + at[0] * 2 + at[2])),
                pl.BlockSpec((HD, HD), lambda i, at: (0, 0)),
            ],
            out_specs=pl.BlockSpec(memory_space=pltpu.VMEM),
        ),
        out_shape=jax.ShapeDtypeStruct((DOCS, 2, CACHE, HD), jnp.bfloat16),
        cost_estimate=pl.CostEstimate(
            flops=8 * DOCS * CACHE * HD * HD, bytes_accessed=8 * DOCS * CACHE * HD, transcendentals=0
        ),
        compiler_params=pltpu.CompilerParams(vmem_limit_bytes=56 * MIB),
        name="turn_cache",
    )(place, cache, cache, had)


PAIR = 2 * ROWS
MOST_PAIRS = 8
SIZES = (4, 2, 1)
BOTH = range(2)


def attend_kernel(
    dx,
    place,
    docs,
    firsts,
    q0_ref,
    q1_ref,
    k_ref,
    v_ref,
    cache_ref,
    o0_ref,
    o1_ref,
    scores,
    acc,
    tops,
    sums,
):
    q_refs, o_refs = (q0_ref, q1_ref), (o0_ref, o1_ref)
    src_x = lax.rem(place[0] + dx, 4)
    scale = np.float32(HD**-0.5 * np.log2(np.e))
    mes = [src_x * 8 + place[1] * 4 + lax.rem(place[2] + n, 2) * 2 + place[3] for n in BOTH]
    first = [firsts[me] for me in mes]
    doc = [docs[me] for me in mes]
    before = [mes[n] - first[n] for n in BOTH]
    pairs = [before[n] // 2 for n in BOTH]
    beside = [jnp.maximum(me - 1, 0) for me in mes]

    def fold(s):
        return s.reshape(-1, 8, QW)

    def regions(n, work):
        big = SIZES[0]

        def body(i, carry):
            work(n, i * big, big)
            return carry

        lax.fori_loop(0, pairs[n] // big, body, 0)
        done = pairs[n] // big * big
        for size in SIZES[1:]:
            need = (pairs[n] & size) != 0

            @pl.when(need)
            def _(done=done, size=size):
                work(n, done, size)

            done = done + jnp.where(need, size, 0)

    key_at = lax.broadcasted_iota(jnp.int32, (PAIR, QW), 0)
    query_at = lax.broadcasted_iota(jnp.int32, (PAIR, QW), 1) % ROWS + ROWS
    causal = key_at <= query_at
    for n in BOTH:
        keys = jnp.concatenate([k_ref[beside[n]], k_ref[mes[n]]], axis=0)
        lowest = jnp.where(before[n] % 2 == 1, 0, ROWS)
        s_own = dot(keys, q_refs[n][...], ((1,), (0,)))
        s_own = jnp.where(causal & (key_at >= lowest), s_own, -jnp.inf)
        scores[n, 1] = s_own
        tops[n] = jnp.max(fold(s_own), axis=0)

    def look(n, begin_at, count):
        best = tops[n]
        for j in range(count):
            i = begin_at + j
            keys = k_ref[pl.ds(first[n] + 2 * i, 2)].reshape(PAIR, HD)
            s = dot(keys, q_refs[n][...], ((1,), (0,)))
            scores[n, 2 + i] = s
            best = jnp.maximum(best, jnp.max(fold(s), axis=0))
        tops[n] = best

    for n in BOTH:
        regions(n, look)

    for n in BOTH:
        s_cache = dot(cache_ref[doc[n], 0], q_refs[n][...], ((1,), (0,)))
        scores[n, 0] = s_cache
        top = jnp.maximum(tops[n], jnp.max(fold(s_cache), axis=0))
        tops[n] = jnp.broadcast_to(jnp.max(top, axis=0, keepdims=True) * scale, (8, QW))

    def weigh(n, i, top):
        p = jnp.exp2(scores[n, i] * scale - top)
        return p.astype(jnp.bfloat16), jnp.sum(fold(p), axis=0)

    for n in BOTH:
        top = tops[n, 0:1]
        p_cache, l_cache = weigh(n, 0, top)
        p_own, l_own = weigh(n, 1, top)
        values = jnp.concatenate([v_ref[beside[n]], v_ref[mes[n]]], axis=1)
        cached = jnp.concatenate(
            [cache_ref[doc[n], 1, :HD], cache_ref[doc[n], 1, HD:]], axis=1
        )
        acc[n] = dot(cached, p_cache, ((1,), (0,))) + dot(values, p_own, ((1,), (0,)))
        sums[n] = l_cache + l_own

    def add(n, begin_at, count):
        top = tops[n, 0:1]
        total = sums[n]
        out = acc[n]
        for j in range(count):
            i = begin_at + j
            p, l = weigh(n, 2 + i, top)
            at = first[n] + 2 * i
            values = jnp.concatenate([v_ref[at], v_ref[at + 1]], axis=1)
            out = out + dot(values, p, ((1,), (0,)))
            total = total + l
        sums[n] = total
        acc[n] = out

    for n in BOTH:
        regions(n, add)

    for n in BOTH:
        out = acc[n] * (1.0 / jnp.sum(sums[n], axis=0, keepdims=True))
        for g in range(GROUP):
            lanes = slice(g * HD, (g + 1) * HD)
            o_refs[n][:, lanes] = out[:, lanes].astype(jnp.bfloat16).T


def attend(dx, place, docs, firsts, q0, q1, keys, values, cache):
    whole = pl.BlockSpec(memory_space=pltpu.VMEM)
    return pl.pallas_call(
        functools.partial(attend_kernel, dx),
        grid_spec=pltpu.PrefetchScalarGridSpec(
            num_scalar_prefetch=3,
            grid=(1,),
            in_specs=[whole] * 5,
            out_specs=[whole, whole],
            scratch_shapes=[
                pltpu.VMEM((2, 2 + MOST_PAIRS, PAIR, QW), jnp.float32),
                pltpu.VMEM((2, HD, QW), jnp.float32),
                pltpu.VMEM((2, 8, QW), jnp.float32),
                pltpu.VMEM((2, 8, QW), jnp.float32),
            ],
        ),
        out_shape=[jax.ShapeDtypeStruct((ROWS, QW), jnp.bfloat16)] * 2,
        cost_estimate=pl.CostEstimate(
            flops=48 * PAIR * QW * HD,
            bytes_accessed=8 * ROWS * QW,
            transcendentals=12 * PAIR * QW,
        ),
        compiler_params=pltpu.CompilerParams(vmem_limit_bytes=20 * MIB),
        name="attend",
    )(place, docs, firsts, q0, q1, keys, values, cache)


def join_kernel(places, place, *refs):
    pieces, out, sem = refs[: len(places)], refs[-2], refs[-1]
    copies = []
    for i, (dx, dl) in enumerate(places):
        head = lax.rem(place[0] + 4 - dx, 4) * 2 + lax.rem(place[2] + dl, 2)
        lanes = pl.ds(pl.multiple_of(head * QW, QW), QW)
        copies.append(pltpu.make_async_copy(pieces[i], out.at[:, lanes], sem.at[i]))
    for copy in copies:
        copy.start()
    for copy in copies:
        copy.wait()


def join(place, places, pieces, base):
    whole = pl.BlockSpec(memory_space=pltpu.VMEM)
    there = pl.BlockSpec(memory_space=pl.ANY)
    known = [] if base is None else [base]
    return pl.pallas_call(
        functools.partial(join_kernel, places),
        grid_spec=pltpu.PrefetchScalarGridSpec(
            num_scalar_prefetch=1,
            grid=(1,),
            in_specs=[whole] * len(pieces) + [there] * len(known),
            out_specs=there,
            scratch_shapes=[pltpu.SemaphoreType.DMA((len(pieces),))],
        ),
        out_shape=jax.ShapeDtypeStruct((ROWS, KVH * QW), jnp.bfloat16),
        input_output_aliases={} if base is None else {1 + len(pieces): 0},
        compiler_params=pltpu.CompilerParams(vmem_limit_bytes=4 * MIB),
        name="join",
    )(place, *pieces, *known)


def out_route(sections, dx, dl):
    route = []
    for z in range(sections):
        for x in range(4):
            for l in range(2):
                target = ((z + 1) % sections, (x + dx) % 4, l ^ dl)
                route.append(((z * 4 + x) * 2 + l, (target[0] * 4 + target[1]) * 2 + target[2]))
    return route


def query_route(dx, dl):
    return [
        (x * 2 + l, (x + 4 - dx) % 4 * 2 + (l ^ dl)) for x in range(4) for l in range(2)
    ]


def per_device(queries, keys_new, values_new, stretch_cache, hadamard_signs, stretch_docs):
    place = jnp.stack([lax.axis_index(name) for name in CTX]).astype(jnp.int32)
    sections = lax.axis_size("section")
    had = jnp.asarray(hadamard(HD), dtype=jnp.bfloat16)
    signs = hadamard_signs[0].astype(jnp.bfloat16)
    kv = pack_kv(keys_new[0], values_new[0])
    mine = lax.all_to_all(kv.reshape(N_CTX, ROWS, HD), CTX, 0, 0, tiled=True)
    q = dict(zip(offsets(), pack_q(place, queries[0])))

    def send(at):
        return lax.ppermute(q[at], ("x", "l"), query_route(*at))

    q[0, 1] = send((0, 1))
    for dx in EARLY:
        q[dx, 0], q[dx, 1] = send((dx, 0)), send((dx, 1))
    cache = turn_cache(place, stretch_cache, had)
    sign_rows = jnp.tile(signs[1], CACHE // HD)[:, None]
    pattern = jnp.stack(
        [jnp.broadcast_to(signs[0], (CACHE, HD)), jnp.broadcast_to(sign_rows, (CACHE, HD))]
    )
    mine, q, cache, pattern = lax.optimization_barrier((mine, q, cache, pattern))
    cache = cache * pattern
    other = lax.ppermute(mine, "c", [(0, 1), (1, 0)])
    for dx in LATE:
        q[dx, 0], q[dx, 1] = send((dx, 0)), send((dx, 1))
    earlier = stretch_docs[None, :] < stretch_docs[:, None]
    firsts = jnp.sum(earlier, axis=1, dtype=jnp.int32)
    keys = jnp.where(place[3] == 0, mine, other)
    values = jnp.where(place[3] == 0, other, mine)
    result = None
    for group in GROUPS:
        outs = {}
        for dx in group:
            outs[dx] = attend(
                dx, place, stretch_docs, firsts, q[dx, 0], q[dx, 1], keys, values, cache
            )
        places = [(dx, dl) for dx in reversed(group) for dl in range(2)]
        outs = lax.optimization_barrier([outs[dx][dl] for dx, dl in places])
        pieces = [
            lax.ppermute(out, ("section", "x", "l"), out_route(sections, dx, dl))
            for out, (dx, dl) in zip(outs, places)
        ]
        split = len(pieces) - 2
        if split:
            result = join(place, places[:split], pieces[:split], result)
        result = join(place, places[split:], pieces[split:], result)
    return result[None]


def solution(mesh):
    sections = mesh.shape["section"]
    split = Mesh(mesh.devices.reshape(sections, 4, 2, 2, 2), ("section",) + CTX)
    rows = P("section", CTX, None)
    in_specs = (rows, rows, rows, P("section", None, None), P("section", None, None), P())
    return jax.shard_map(
        per_device, mesh=split, in_specs=in_specs, out_specs=rows, check_vma=False
    )
```

time: 90.6 us -> 89.3 us (0.986)
  the two profiles are of different devices: /device:TPU:26 before, /device:TPU:3 now
where the time goes in v2:
time: 89.3 us; the launch traced here: 88.7 us
  starting transfers between devices  37.3 us (42%)
  Pallas kernels  26.1 us (29%)
  waiting for transfers between devices  21.8 us (24%)
  other arithmetic  2.96 us (3%)
    ppermute x8, starting transfers between devices, per_device(): lax.ppermute(out, ('section', 'x', 'l'), out_route(sections, dx, dl))  20.5 us
    pallas_call x4, Pallas kernels, attend(): pl.pallas_call(functools.partial(attend_kernel, dx), grid_spec=pltpu.Pref...  12.5 us
    ppermute x7, waiting for transfers between devices, send(): return lax.ppermute(q[at], ('x', 'l'), query_route(*at))  11.7 us
    ppermute x8, waiting for transfers between devices, per_device(): lax.ppermute(out, ('section', 'x', 'l'), out_route(sections, dx, dl))  9.46 us
    ppermute x7, starting transfers between devices, send(): return lax.ppermute(q[at], ('x', 'l'), query_route(*at))  7.95 us
    all_to_all x1, starting transfers between devices, per_device(): mine = lax.all_to_all(kv.reshape(N_CTX, ROWS, HD), CTX, 0, 0, tiled=True)  7.94 us
    pallas_call x4, Pallas kernels, join(): pl.pallas_call(functools.partial(join_kernel, places), grid_spec=pltpu.Pr...  5.06 us
    pallas_call x1, Pallas kernels, turn_cache(): pl.pallas_call(turn_kernel, grid_spec=pltpu.PrefetchScalarGridSpec(num_sc...  3.45 us
  transfers between devices with their start and end apart: 17, of which 8 were waited for; matrix products, arithmetic and copies ran while one was open for 3% of the time, Pallas kernels for 26%

profile of v2, /device:TPU:3, one launch (start us, length us, event | category | flops | bytes accessed | tf_op | source)
XLA Modules:
  0.0 88.7 jit_solution(18163372720513926446)
XLA Ops:
  0.0 2.0 %pack_kv.1 = bf16[4,2,2,2,128,128]{5,4,3,2,1,0:T(8,128)(2,1)} custom-call(bf16[128,1024]{1,0:T(8,128)(2,1)} %bitcast.17, bf16[128,1024]{1,0:T(8,128)(2,1)} %bitcast.18), custom_call_target="tpu_custom_call" | custom-call | bytes 1572864 | tf_op jit(solution)/shard_map/pack_kv/pallas_call | solution.py:85
  2.0 7.9 %all-to-all-start = ((bf16[32,128,128]{2,1,0:T(8,128)(2,1)}), bf16[32,128,128]{2,1,0:T(8,128)(2,1)S(1)}, u32[]{:S(2)}, u32[]{:S(2)}) async-start(bf16[32,128,128]{2,1,0:T(8,128)(2,1)} %bitcast.15), calls=%async_computation | async-start | bytes 2097152 | tf_op jit(solution)/shard_map/all_to_all | solution.py:338
  10.0 0.6 pad_add_fusion.place
  10.6 3.1 %pack_q.1 = (bf16[128,512]{1,0:T(8,128)(2,1)}, bf16[128,512]{1,0:T(8,128)(2,1)}, bf16[128,512]{1,0:T(8,128)(2,1)}, bf16[128,512]{1,0:T(8,128)(2,1)}, bf16[128,51...) custom-call(s32[4]{0:T(128)} %pad_add_fusion.place, ...), custom_call_target="tpu_custom_call" | custom-call | bytes 2097152 | tf_op jit(solution)/shard_map/pack_q/pallas_call | solution.py:56
  13.7 1.2 %collective-permute-start = (bf16[128,512]{1,0:T(8,128)(2,1)}, bf16[128,512]{1,0:T(8,128)(2,1)S(1)}, u32[]{:S(2)}, u32[]{:S(2)}) collective-permute-start(bf16[128,512]{1,0:T(8,128)(2,1)} %get-tuple-element.37), channel_id=1, source_target_pairs={{0,2},{2,0},{8,10},{10,8},{16,18},{18,16},{24,26},{26,24},{1,3},{3... | collective-permute-start | bytes 393224 | tf_op jit(solution)/shard_map/ppermute | solution.py:342
  14.8 0.3 collective-permute-start.1
  15.1 2.4 %collective-permute-start.2 = (bf16[128,512]{1,0:T(8,128)(2,1)}, bf16[128,512]{1,0:T(8,128)(2,1)S(1)}, u32[]{:S(2)}, u32[]{:S(2)}) collective-permute-start(bf16[128,512]{1,0:T(8,128)(2,1)} %get-tuple-element.39), channel_id=1, source_target_pairs={{0,26},{2,24},{8,2},{10,0},{16,10},{18,8},{24,18},{26,16},{1,27},{... | collective-permute-start | bytes 393224 | tf_op jit(solution)/shard_map/ppermute | solution.py:342
  17.6 3.9 %collective-permute-start.4 = (bf16[128,512]{1,0:T(8,128)(2,1)}, bf16[128,512]{1,0:T(8,128)(2,1)S(1)}, u32[]{:S(2)}, u32[]{:S(2)}) collective-permute-start(bf16[128,512]{1,0:T(8,128)(2,1)} %get-tuple-element.41), channel_id=1, source_target_pairs={{0,18},{2,16},{8,26},{10,24},{16,2},{18,0},{24,10},{26,8},{1,19},{... | collective-permute-start | bytes 393224 | tf_op jit(solution)/shard_map/ppermute | solution.py:342
  21.4 0.7 convert_element_type.8
  22.2 3.5 %turn_cache.1 = bf16[8,2,256,128]{3,2,1,0:T(8,128)(2,1)} custom-call(s32[4]{0:T(128)} %pad_add_fusion.place, bf16[1,2048,2048]{2,1,0:T(8,128)(2,1)} %cv_ref.1, bf16[1,2048,2048]{2,1,0:T(8,128)(2,1)} %cv_ref.1, bf16[128,128]{1,0:T(8,128)(2,1)} %constant.18.clone.had_ref), custom_call_target="tpu_custom_call" | custom-call | flops 268435456 | bytes 2097152 | tf_op jit(solution)/shard_map/turn_cache/pallas_call | solution.py:112
  25.8 0.7 collective-permute-done.q1_ref
  26.5 3.3 %collective-permute-done.2.q1_ref = bf16[128,512]{1,0:T(8,128)(2,1)S(1)} collective-permute-done((bf16[128,512]{1,0:T(8,128)(2,1)}, bf16[128,512]{1,0:T(8,128)(2,1)S(1)}, u32[]{:S(2)}, u32[]{:S(2)}) %collective-permute-start.2) | collective-permute-done | bytes 131104 | tf_op jit(solution)/shard_map/ppermute | solution.py:342
  29.8 4.1 %collective-permute-done.3.q0_ref = bf16[128,512]{1,0:T(8,128)(2,1)S(1)} collective-permute-done((bf16[128,512]{1,0:T(8,128)(2,1)}, bf16[128,512]{1,0:T(8,128)(2,1)S(1)}, u32[]{:S(2)}, u32[]{:S(2)}) %collective-permute-start.3) | collective-permute-done | bytes 131104 | tf_op jit(solution)/shard_map/ppermute | solution.py:342
  33.9 3.6 %collective-permute-done.4.q1_ref = bf16[128,512]{1,0:T(8,128)(2,1)S(1)} collective-permute-done((bf16[128,512]{1,0:T(8,128)(2,1)}, bf16[128,512]{1,0:T(8,128)(2,1)S(1)}, u32[]{:S(2)}, u32[]{:S(2)}) %collective-permute-start.4) | collective-permute-done | bytes 131104 | tf_op jit(solution)/shard_map/ppermute | solution.py:342
  37.5 0.9 collective-permute-start.7
  38.8 1.3 %broadcast_multiply_fusion.cache_ref = bf16[8,2,256,128]{3,2,1,0:T(8,128)(2,1)S(1)} fusion(bf16[8,2,256,128]{3,2,1,0:T(8,128)(2,1)} %turn_cache.1, bf16[2,256,128]{2,1,0:T(8,128)(2,1)S(1)} %pad_maximum_fusion), kind=kLoop, calls=%fused_computation.2 | loop fusion | flops 524288 | bytes 2228224 | tf_op jit(solution)/shard_map/mul | solution.py:353
  40.1 0.6 collective-permute-done.7
  40.8 3.5 %attend.7 = (bf16[128,512]{1,0:T(8,128)(2,1)S(1)}, bf16[128,512]{1,0:T(8,128)(2,1)S(1)}) custom-call(s32[4]{0:T(128)S(1)} %copy-done.1, s32[32]{0:T(128)S(1)} %copy-done.2, s32[32]{0:T(128)S(1)} %convert_reduce_fusion.firsts, bf16[128,512]{1,0:T(8,128)(2,1)S(1)} %copy-done, bf16[128,512]{1,0:T(8,128)(2,1)S(1)} %collective-permute-done.q1_ref, ...), custom_call_target="tpu_custom_call" | custom-call | flops 805306368 | bytes 524288 | tf_op jit(solution)/shard_map/attend/pallas_call | solution.py:258
  44.3 1.7 %collective-permute-start.14 = (bf16[128,512]{1,0:T(8,128)(2,1)S(1)}, bf16[128,512]{1,0:T(8,128)(2,1)S(1)}, u32[]{:S(2)}, u32[]{:S(2)}) collective-permute-start(bf16[128,512]{1,0:T(8,128)(2,1)S(1)} %get-tuple-element.65), channel_id=1, source_target_pairs={{0,32},{2,34},{8,40},{10,42},{16,48},{18,50},{24,56},{26,58},{32,6... | collective-permute-start | bytes 393224 | tf_op jit(solution)/shard_map/ppermute | solution.py:371
  46.0 1.9 %collective-permute-start.15 = (bf16[128,512]{1,0:T(8,128)(2,1)S(1)}, bf16[128,512]{1,0:T(8,128)(2,1)S(1)}, u32[]{:S(2)}, u32[]{:S(2)}) collective-permute-start(bf16[128,512]{1,0:T(8,128)(2,1)S(1)} %get-tuple-element.66), channel_id=1, source_target_pairs={{0,34},{2,32},{8,42},{10,40},{16,50},{18,48},{24,58},{26,56},{32,6... | collective-permute-start | bytes 393224 | tf_op jit(solution)/shard_map/ppermute | solution.py:371
  48.0 1.8 %attend.6 = (bf16[128,512]{1,0:T(8,128)(2,1)S(1)}, bf16[128,512]{1,0:T(8,128)(2,1)S(1)}) custom-call(s32[4]{0:T(128)S(1)} %copy-done.1, s32[32]{0:T(128)S(1)} %copy-done.2, s32[32]{0:T(128)S(1)} %convert_reduce_fusion.firsts, bf16[128,512]{1,0:T(8,128)(2,1)S(1)} %collective-permute-done.3.q0_ref, bf16[128,512]{1,0:T(8,128)(2,1)S(1)} %collective-permute-done.4.q1_ref, ...), custom_call_target="tpu_custom_call" | custom-call | flops 805306368 | bytes 524288 | tf_op jit(solution)/shard_map/attend/pallas_call | solution.py:258
  49.8 4.6 %collective-permute-start.12 = (bf16[128,512]{1,0:T(8,128)(2,1)S(1)}, bf16[128,512]{1,0:T(8,128)(2,1)S(1)}, u32[]{:S(2)}, u32[]{:S(2)}) collective-permute-start(bf16[128,512]{1,0:T(8,128)(2,1)S(1)} %get-tuple-element.61), channel_id=1, source_target_pairs={{0,48},{2,50},{8,56},{10,58},{16,32},{18,34},{24,40},{26,42},{32,8... | collective-permute-start | bytes 393224 | tf_op jit(solution)/shard_map/ppermute | solution.py:371
  54.4 5.4 %attend.5 = (bf16[128,512]{1,0:T(8,128)(2,1)S(1)}, bf16[128,512]{1,0:T(8,128)(2,1)S(1)}) custom-call(s32[4]{0:T(128)S(1)} %copy-done.1, s32[32]{0:T(128)S(1)} %copy-done.2, s32[32]{0:T(128)S(1)} %convert_reduce_fusion.firsts, bf16[128,512]{1,0:T(8,128)(2,1)S(1)} %collective-permute-done.1.q0_ref, bf16[128,512]{1,0:T(8,128)(2,1)S(1)} %collective-permute-done.2.q1_ref, ...), custom_call_target="tpu_custom_call" | custom-call | flops 805306368 | bytes 524288 | tf_op jit(solution)/shard_map/attend/pallas_call | solution.py:258
  59.9 1.8 %attend.4 = (bf16[128,512]{1,0:T(8,128)(2,1)S(1)}, bf16[128,512]{1,0:T(8,128)(2,1)S(1)}) custom-call(s32[4]{0:T(128)S(1)} %copy-done.1, s32[32]{0:T(128)S(1)} %copy-done.2, s32[32]{0:T(128)S(1)} %convert_reduce_fusion.firsts, bf16[128,512]{1,0:T(8,128)(2,1)S(1)} %collective-permute-done.5.q0_ref, bf16[128,512]{1,0:T(8,128)(2,1)S(1)} %collective-permute-done.6.q1_ref, ...), custom_call_target="tpu_custom_call" | custom-call | flops 805306368 | bytes 524288 | tf_op jit(solution)/shard_map/attend/pallas_call | solution.py:258
  61.7 3.0 %collective-permute-start.10 = (bf16[128,512]{1,0:T(8,128)(2,1)S(1)}, bf16[128,512]{1,0:T(8,128)(2,1)S(1)}, u32[]{:S(2)}, u32[]{:S(2)}) collective-permute-start(bf16[128,512]{1,0:T(8,128)(2,1)S(1)} %get-tuple-element.57), channel_id=1, source_target_pairs={{0,56},{2,58},{8,32},{10,34},{16,40},{18,42},{24,48},{26,50},{32,8... | collective-permute-start | bytes 393224 | tf_op jit(solution)/shard_map/ppermute | solution.py:371
  64.7 9.1 %collective-permute-start.11 = (bf16[128,512]{1,0:T(8,128)(2,1)S(1)}, bf16[128,512]{1,0:T(8,128)(2,1)S(1)}, u32[]{:S(2)}, u32[]{:S(2)}) collective-permute-start(bf16[128,512]{1,0:T(8,128)(2,1)S(1)} %get-tuple-element.58), channel_id=1, source_target_pairs={{0,58},{2,56},{8,34},{10,32},{16,42},{18,40},{24,50},{26,48},{32,9... | collective-permute-start | bytes 393224 | tf_op jit(solution)/shard_map/ppermute | solution.py:371
  73.9 1.3 %join.4.refs_2_ = bf16[128,4096]{1,0:T(8,128)(2,1)} custom-call(s32[4]{0:T(128)S(1)} %copy-done.1, bf16[128,512]{1,0:T(8,128)(2,1)S(1)} %collective-permute-done.14.refs_0_, bf16[128,512]{1,0:T(8,128)(2,1)S(1)} %collective-permute-done.15.refs_1_), custom_call_target="tpu_custom_call" | custom-call | tf_op jit(solution)/shard_map/join/pallas_call | solution.py:300
  75.2 1.3 %join.5.refs_2_ = bf16[128,4096]{1,0:T(8,128)(2,1)} custom-call(s32[4]{0:T(128)S(1)} %copy-done.1, bf16[128,512]{1,0:T(8,128)(2,1)S(1)} %collective-permute-done.12.refs_0_, bf16[128,512]{1,0:T(8,128)(2,1)S(1)} %collective-permute-done.13.refs_1_, bf16[128,4096]{1,0:T(8,128)(2,1)} %join.4.refs_2_), custom_call_target="tpu_custom_call", output_to_operand_aliasing={{}: (3, {})} | custom-call | tf_op jit(solution)/shard_map/join/pallas_call | solution.py:300
  76.6 1.3 %join.6.refs_2_ = bf16[128,4096]{1,0:T(8,128)(2,1)} custom-call(s32[4]{0:T(128)S(1)} %copy-done.1, bf16[128,512]{1,0:T(8,128)(2,1)S(1)} %collective-permute-done.10.refs_0_, bf16[128,512]{1,0:T(8,128)(2,1)S(1)} %collective-permute-done.11.refs_1_, bf16[128,4096]{1,0:T(8,128)(2,1)} %join.5.refs_2_), custom_call_target="tpu_custom_call", output_to_operand_aliasing={{}: (3, {})} | custom-call | tf_op jit(solution)/shard_map/join/pallas_call | solution.py:300
  77.9 5.7 %collective-permute-done.8.refs_0_ = bf16[128,512]{1,0:T(8,128)(2,1)S(1)} collective-permute-done((bf16[128,512]{1,0:T(8,128)(2,1)S(1)}, bf16[128,512]{1,0:T(8,128)(2,1)S(1)}, u32[]{:S(2)}, u32[]{:S(2)}) %collective-permute-start.8) | collective-permute-done | bytes 131104 | tf_op jit(solution)/shard_map/ppermute | solution.py:371
  83.6 3.7 %collective-permute-done.9.refs_1_ = bf16[128,512]{1,0:T(8,128)(2,1)S(1)} collective-permute-done((bf16[128,512]{1,0:T(8,128)(2,1)S(1)}, bf16[128,512]{1,0:T(8,128)(2,1)S(1)}, u32[]{:S(2)}, u32[]{:S(2)}) %collective-permute-start.9) | collective-permute-done | bytes 131104 | tf_op jit(solution)/shard_map/ppermute | solution.py:371
  87.2 1.3 %join.7 = bf16[128,4096]{1,0:T(8,128)(2,1)} custom-call(s32[4]{0:T(128)S(1)} %copy-done.1, bf16[128,512]{1,0:T(8,128)(2,1)S(1)} %collective-permute-done.8.refs_0_, bf16[128,512]{1,0:T(8,128)(2,1)S(1)} %collective-permute-done.9.refs_1_, bf16[128,4096]{1,0:T(8,128)(2,1)} %join.6.refs_2_), custom_call_target="tpu_custom_call", output_to_operand_aliasing={{}: (3, {})} | custom-call | tf_op jit(solution)/shard_map/join/pallas_call | solution.py:300
  (33 shorter events, 0.9 us)
Async XLA Ops:
  2.0 35.5 %all-to-all-start = ((bf16[32,128,128]{2,1,0:T(8,128)(2,1)}), bf16[32,128,128]{2,1,0:T(8,128)(2,1)S(1)}, u32[]{:S(2)}, u32[]{:S(2)}) async-start(bf16[32,128,128]{2,1,0:T(8,128)(2,1)} %bitcast.15), calls=%async_computation | async-start | bytes 2097152 | tf_op jit(solution)/shard_map/all_to_all | solution.py:338
  13.7 12.8 %collective-permute-start = (bf16[128,512]{1,0:T(8,128)(2,1)}, bf16[128,512]{1,0:T(8,128)(2,1)S(1)}, u32[]{:S(2)}, u32[]{:S(2)}) collective-permute-start(bf16[128,512]{1,0:T(8,128)(2,1)} %get-tuple-element.37), channel_id=1, source_target_pairs={{0,2},{2,0},{8,10},{10,8},{16,18},{18,16},{24,26},{26,24},{1,3},{3... | collective-permute-start | bytes 393224 | tf_op jit(solution)/shard_map/ppermute | solution.py:342
  14.8 11.6 %collective-permute-start.1 = (bf16[128,512]{1,0:T(8,128)(2,1)}, bf16[128,512]{1,0:T(8,128)(2,1)S(1)}, u32[]{:S(2)}, u32[]{:S(2)}) collective-permute-start(bf16[128,512]{1,0:T(8,128)(2,1)} %get-tuple-element.38), channel_id=1, source_target_pairs={{0,24},{2,26},{8,0},{10,2},{16,8},{18,10},{24,16},{26,18},{1,25},{... | collective-permute-start | bytes 393224 | tf_op jit(solution)/shard_map/ppermute | solution.py:342
  15.1 14.7 %collective-permute-start.2 = (bf16[128,512]{1,0:T(8,128)(2,1)}, bf16[128,512]{1,0:T(8,128)(2,1)S(1)}, u32[]{:S(2)}, u32[]{:S(2)}) collective-permute-start(bf16[128,512]{1,0:T(8,128)(2,1)} %get-tuple-element.39), channel_id=1, source_target_pairs={{0,26},{2,24},{8,2},{10,0},{16,10},{18,8},{24,18},{26,16},{1,27},{... | collective-permute-start | bytes 393224 | tf_op jit(solution)/shard_map/ppermute | solution.py:342
  17.6 16.3 %collective-permute-start.3 = (bf16[128,512]{1,0:T(8,128)(2,1)}, bf16[128,512]{1,0:T(8,128)(2,1)S(1)}, u32[]{:S(2)}, u32[]{:S(2)}) collective-permute-start(bf16[128,512]{1,0:T(8,128)(2,1)} %get-tuple-element.40), channel_id=1, source_target_pairs={{0,16},{2,18},{8,24},{10,26},{16,0},{18,2},{24,8},{26,10},{1,17},{... | collective-permute-start | bytes 393224 | tf_op jit(solution)/shard_map/ppermute | solution.py:342
  17.6 19.9 %collective-permute-start.4 = (bf16[128,512]{1,0:T(8,128)(2,1)}, bf16[128,512]{1,0:T(8,128)(2,1)S(1)}, u32[]{:S(2)}, u32[]{:S(2)}) collective-permute-start(bf16[128,512]{1,0:T(8,128)(2,1)} %get-tuple-element.41), channel_id=1, source_target_pairs={{0,18},{2,16},{8,26},{10,24},{16,2},{18,0},{24,10},{26,8},{1,19},{... | collective-permute-start | bytes 393224 | tf_op jit(solution)/shard_map/ppermute | solution.py:342
  22.1 16.2 %copy-start.2 = (s32[32]{0:T(128)S(1)}, s32[32]{0:T(128)}, u32[]{:S(2)}) copy-start(s32[32]{0:T(128)} %docs.7) | copy-start | bytes 388
  22.1 16.4 %copy-start.4 = (bf16[128,512]{1,0:T(8,128)(2,1)S(1)}, bf16[128,512]{1,0:T(8,128)(2,1)}, u32[]{:S(2)}) copy-start(bf16[128,512]{1,0:T(8,128)(2,1)} %get-tuple-element.44) | copy-start | bytes 393220
  22.2 16.5 %copy-start.3 = (bf16[128,512]{1,0:T(8,128)(2,1)S(1)}, bf16[128,512]{1,0:T(8,128)(2,1)}, u32[]{:S(2)}) copy-start(bf16[128,512]{1,0:T(8,128)(2,1)} %get-tuple-element.45) | copy-start | bytes 393220
  22.2 18.6 %copy-start = (bf16[128,512]{1,0:T(8,128)(2,1)S(1)}, bf16[128,512]{1,0:T(8,128)(2,1)}, u32[]{:S(2)}) copy-start(bf16[128,512]{1,0:T(8,128)(2,1)} %get-tuple-element.63.q0_ref) | copy-start | bytes 393220
  22.2 18.6 %copy-start.1 = (s32[4]{0:T(128)S(1)}, s32[4]{0:T(128)}, u32[]{:S(2)}) copy-start(s32[4]{0:T(128)} %pad_add_fusion.place) | copy-start | bytes 52
  37.5 3.2 %collective-permute-start.7 = (bf16[32,128,128]{2,1,0:T(8,128)(2,1)S(1)}, bf16[32,128,128]{2,1,0:T(8,128)(2,1)S(1)}, u32[]{:S(2)}, u32[]{:S(2)}) collective-permute-start(bf16[32,128,128]{2,1,0:T(8,128)(2,1)S(1)} %all-to-all-done), channel_id=1, source_target_pairs={{0,1},{1,0},{2,3},{3,2},{4,5},{5,4},{6,7},{7,6},{8,9},{9,8},{10,11... | collective-permute-start | bytes 3145736 | tf_op jit(solution)/shard_map/ppermute | solution.py:354
  38.6 21.2 %collective-permute-start.5 = (bf16[128,512]{1,0:T(8,128)(2,1)S(1)}, bf16[128,512]{1,0:T(8,128)(2,1)S(1)}, u32[]{:S(2)}, u32[]{:S(2)}) collective-permute-start(bf16[128,512]{1,0:T(8,128)(2,1)S(1)} %copy-done.4), channel_id=1, source_target_pairs={{0,8},{2,10},{8,16},{10,18},{16,24},{18,26},{24,0},{26,2},{1,9},{3... | collective-permute-start | bytes 393224 | tf_op jit(solution)/shard_map/ppermute | solution.py:342
  38.7 21.2 %collective-permute-start.6 = (bf16[128,512]{1,0:T(8,128)(2,1)S(1)}, bf16[128,512]{1,0:T(8,128)(2,1)S(1)}, u32[]{:S(2)}, u32[]{:S(2)}) collective-permute-start(bf16[128,512]{1,0:T(8,128)(2,1)S(1)} %copy-done.3), channel_id=1, source_target_pairs={{0,10},{2,8},{8,18},{10,16},{16,26},{18,24},{24,2},{26,0},{1,11},{... | collective-permute-start | bytes 393224 | tf_op jit(solution)/shard_map/ppermute | solution.py:342
  44.3 20.4 %collective-permute-start.14 = (bf16[128,512]{1,0:T(8,128)(2,1)S(1)}, bf16[128,512]{1,0:T(8,128)(2,1)S(1)}, u32[]{:S(2)}, u32[]{:S(2)}) collective-permute-start(bf16[128,512]{1,0:T(8,128)(2,1)S(1)} %get-tuple-element.65), channel_id=1, source_target_pairs={{0,32},{2,34},{8,40},{10,42},{16,48},{18,50},{24,56},{26,58},{32,6... | collective-permute-start | bytes 393224 | tf_op jit(solution)/shard_map/ppermute | solution.py:371
  46.0 27.8 %collective-permute-start.15 = (bf16[128,512]{1,0:T(8,128)(2,1)S(1)}, bf16[128,512]{1,0:T(8,128)(2,1)S(1)}, u32[]{:S(2)}, u32[]{:S(2)}) collective-permute-start(bf16[128,512]{1,0:T(8,128)(2,1)S(1)} %get-tuple-element.66), channel_id=1, source_target_pairs={{0,34},{2,32},{8,42},{10,40},{16,50},{18,48},{24,58},{26,56},{32,6... | collective-permute-start | bytes 393224 | tf_op jit(solution)/shard_map/ppermute | solution.py:371
  49.8 24.0 %collective-permute-start.12 = (bf16[128,512]{1,0:T(8,128)(2,1)S(1)}, bf16[128,512]{1,0:T(8,128)(2,1)S(1)}, u32[]{:S(2)}, u32[]{:S(2)}) collective-permute-start(bf16[128,512]{1,0:T(8,128)(2,1)S(1)} %get-tuple-element.61), channel_id=1, source_target_pairs={{0,48},{2,50},{8,56},{10,58},{16,32},{18,34},{24,40},{26,42},{32,8... | collective-permute-start | bytes 393224 | tf_op jit(solution)/shard_map/ppermute | solution.py:371
  59.8 15.4 %collective-permute-start.13 = (bf16[128,512]{1,0:T(8,128)(2,1)S(1)}, bf16[128,512]{1,0:T(8,128)(2,1)S(1)}, u32[]{:S(2)}, u32[]{:S(2)}) collective-permute-start(bf16[128,512]{1,0:T(8,128)(2,1)S(1)} %get-tuple-element.62), channel_id=1, source_target_pairs={{0,50},{2,48},{8,58},{10,56},{16,34},{18,32},{24,42},{26,40},{32,8... | collective-permute-start | bytes 393224 | tf_op jit(solution)/shard_map/ppermute | solution.py:371
  61.7 14.7 %collective-permute-start.10 = (bf16[128,512]{1,0:T(8,128)(2,1)S(1)}, bf16[128,512]{1,0:T(8,128)(2,1)S(1)}, u32[]{:S(2)}, u32[]{:S(2)}) collective-permute-start(bf16[128,512]{1,0:T(8,128)(2,1)S(1)} %get-tuple-element.57), channel_id=1, source_target_pairs={{0,56},{2,58},{8,32},{10,34},{16,40},{18,42},{24,48},{26,50},{32,8... | collective-permute-start | bytes 393224 | tf_op jit(solution)/shard_map/ppermute | solution.py:371
  64.7 11.8 %collective-permute-start.11 = (bf16[128,512]{1,0:T(8,128)(2,1)S(1)}, bf16[128,512]{1,0:T(8,128)(2,1)S(1)}, u32[]{:S(2)}, u32[]{:S(2)}) collective-permute-start(bf16[128,512]{1,0:T(8,128)(2,1)S(1)} %get-tuple-element.58), channel_id=1, source_target_pairs={{0,58},{2,56},{8,34},{10,32},{16,42},{18,40},{24,50},{26,48},{32,9... | collective-permute-start | bytes 393224 | tf_op jit(solution)/shard_map/ppermute | solution.py:371
  73.8 9.7 %collective-permute-start.8 = (bf16[128,512]{1,0:T(8,128)(2,1)S(1)}, bf16[128,512]{1,0:T(8,128)(2,1)S(1)}, u32[]{:S(2)}, u32[]{:S(2)}) collective-permute-start(bf16[128,512]{1,0:T(8,128)(2,1)S(1)} %get-tuple-element.55), channel_id=1, source_target_pairs={{0,40},{2,42},{8,48},{10,50},{16,56},{18,58},{24,32},{26,34},{32,7... | collective-permute-start | bytes 393224 | tf_op jit(solution)/shard_map/ppermute | solution.py:371
  73.8 13.4 %collective-permute-start.9 = (bf16[128,512]{1,0:T(8,128)(2,1)S(1)}, bf16[128,512]{1,0:T(8,128)(2,1)S(1)}, u32[]{:S(2)}, u32[]{:S(2)}) collective-permute-start(bf16[128,512]{1,0:T(8,128)(2,1)S(1)} %get-tuple-element.56), channel_id=1, source_target_pairs={{0,42},{2,40},{8,50},{10,48},{16,58},{18,56},{24,34},{26,32},{32,7... | collective-permute-start | bytes 393224 | tf_op jit(solution)/shard_map/ppermute | solution.py:371

commit v3 on v2

--- a/solution.py
+++ b/solution.py
@@ -18,9 +18,9 @@
 DOCS = 8
 QW = GROUP * HD
 MIB = 1024 * 1024
-EARLY = (2, 1)
-LATE = (3,)
-GROUPS = ((0,), (2,), (1, 3))
+EARLY = (1, 3)
+LATE = (2,)
+GROUPS = ((0,), (1, 3, 2))
 
 CTX = ("x", "h", "l", "c")
 

time: 89.3 us -> 81.3 us (0.910)
  the two profiles are of different devices: /device:TPU:3 before, /device:TPU:26 now
where the time goes in v3:
time: 81.3 us; the launch traced here: 80.8 us
  starting transfers between devices  35.9 us (44%)
  Pallas kernels  25.4 us (31%)
  waiting for transfers between devices  16 us (20%)
  other arithmetic  2.96 us (4%)
    ppermute x8, starting transfers between devices, per_device(): lax.ppermute(out, ('section', 'x', 'l'), out_route(sections, dx, dl))  18.4 us
    pallas_call x4, Pallas kernels, attend(): pl.pallas_call(functools.partial(attend_kernel, dx), grid_spec=pltpu.Pref...  12.9 us
    ppermute x7, starting transfers between devices, send(): return lax.ppermute(q[at], ('x', 'l'), query_route(*at))  10.2 us
    ppermute x8, waiting for transfers between devices, per_device(): lax.ppermute(out, ('section', 'x', 'l'), out_route(sections, dx, dl))  8.26 us
    ppermute x7, waiting for transfers between devices, send(): return lax.ppermute(q[at], ('x', 'l'), query_route(*at))  7.77 us
    all_to_all x1, starting transfers between devices, per_device(): mine = lax.all_to_all(kv.reshape(N_CTX, ROWS, HD), CTX, 0, 0, tiled=True)  7.28 us
    pallas_call x3, Pallas kernels, join(): pl.pallas_call(functools.partial(join_kernel, places), grid_spec=pltpu.Pr...  3.89 us
    pallas_call x1, Pallas kernels, turn_cache(): pl.pallas_call(turn_kernel, grid_spec=pltpu.PrefetchScalarGridSpec(num_sc...  3.45 us
  transfers between devices with their start and end apart: 17, of which 7 were waited for; matrix products, arithmetic and copies ran while one was open for 4% of the time, Pallas kernels for 27%

profile of v3, /device:TPU:26, one launch (start us, length us, event | category | flops | bytes accessed | tf_op | source)
XLA Modules:
  0.0 80.8 jit_solution(6219376234455760231)
XLA Ops:
  0.0 2.0 %pack_kv.1 = bf16[4,2,2,2,128,128]{5,4,3,2,1,0:T(8,128)(2,1)} custom-call(bf16[128,1024]{1,0:T(8,128)(2,1)} %bitcast.17, bf16[128,1024]{1,0:T(8,128)(2,1)} %bitcast.18), custom_call_target="tpu_custom_call" | custom-call | bytes 1572864 | tf_op jit(solution)/shard_map/pack_kv/pallas_call | solution.py:85
  2.0 7.3 %all-to-all-start = ((bf16[32,128,128]{2,1,0:T(8,128)(2,1)}), bf16[32,128,128]{2,1,0:T(8,128)(2,1)S(1)}, u32[]{:S(2)}, u32[]{:S(2)}) async-start(bf16[32,128,128]{2,1,0:T(8,128)(2,1)} %bitcast.15), calls=%async_computation | async-start | bytes 2097152 | tf_op jit(solution)/shard_map/all_to_all | solution.py:338
  10.0 3.1 %pack_q.1 = (bf16[128,512]{1,0:T(8,128)(2,1)}, bf16[128,512]{1,0:T(8,128)(2,1)}, bf16[128,512]{1,0:T(8,128)(2,1)}, bf16[128,512]{1,0:T(8,128)(2,1)}, bf16[128,51...) custom-call(s32[4]{0:T(128)} %pad_add_fusion.place, ...), custom_call_target="tpu_custom_call" | custom-call | bytes 2097152 | tf_op jit(solution)/shard_map/pack_q/pallas_call | solution.py:56
  13.0 0.9 %collective-permute-start = (bf16[128,512]{1,0:T(8,128)(2,1)}, bf16[128,512]{1,0:T(8,128)(2,1)S(1)}, u32[]{:S(2)}, u32[]{:S(2)}) collective-permute-start(bf16[128,512]{1,0:T(8,128)(2,1)} %get-tuple-element.39), channel_id=1, source_target_pairs={{0,2},{2,0},{8,10},{10,8},{16,18},{18,16},{24,26},{26,24},{1,3},{3... | collective-permute-start | bytes 393224 | tf_op jit(solution)/shard_map/ppermute | solution.py:342
  14.4 3.4 %collective-permute-start.2 = (bf16[128,512]{1,0:T(8,128)(2,1)}, bf16[128,512]{1,0:T(8,128)(2,1)S(1)}, u32[]{:S(2)}, u32[]{:S(2)}) collective-permute-start(bf16[128,512]{1,0:T(8,128)(2,1)} %get-tuple-element.41), channel_id=1, source_target_pairs={{0,26},{2,24},{8,2},{10,0},{16,10},{18,8},{24,18},{26,16},{1,27},{... | collective-permute-start | bytes 393224 | tf_op jit(solution)/shard_map/ppermute | solution.py:342
  17.8 1.0 %collective-permute-start.4 = (bf16[128,512]{1,0:T(8,128)(2,1)}, bf16[128,512]{1,0:T(8,128)(2,1)S(1)}, u32[]{:S(2)}, u32[]{:S(2)}) collective-permute-start(bf16[128,512]{1,0:T(8,128)(2,1)} %get-tuple-element.45), channel_id=1, source_target_pairs={{0,10},{2,8},{8,18},{10,16},{16,26},{18,24},{24,2},{26,0},{1,11},{... | collective-permute-start | bytes 393224 | tf_op jit(solution)/shard_map/ppermute | solution.py:342
  18.8 0.7 convert_element_type.8
  19.6 3.5 %turn_cache.1 = bf16[8,2,256,128]{3,2,1,0:T(8,128)(2,1)} custom-call(s32[4]{0:T(128)} %pad_add_fusion.place, bf16[1,2048,2048]{2,1,0:T(8,128)(2,1)} %cv_ref.1, bf16[1,2048,2048]{2,1,0:T(8,128)(2,1)} %cv_ref.1, bf16[128,128]{1,0:T(8,128)(2,1)} %constant.18.clone.had_ref), custom_call_target="tpu_custom_call" | custom-call | flops 268435456 | bytes 2097152 | tf_op jit(solution)/shard_map/turn_cache/pallas_call | solution.py:112
  23.2 2.6 %collective-permute-done.q1_ref = bf16[128,512]{1,0:T(8,128)(2,1)S(1)} collective-permute-done((bf16[128,512]{1,0:T(8,128)(2,1)}, bf16[128,512]{1,0:T(8,128)(2,1)S(1)}, u32[]{:S(2)}, u32[]{:S(2)}) %collective-permute-start) | collective-permute-done | bytes 131104 | tf_op jit(solution)/shard_map/ppermute | solution.py:342
  25.8 0.6 collective-permute-done.1.q0_ref
  26.4 4.5 %collective-permute-done.2.q1_ref = bf16[128,512]{1,0:T(8,128)(2,1)S(1)} collective-permute-done((bf16[128,512]{1,0:T(8,128)(2,1)}, bf16[128,512]{1,0:T(8,128)(2,1)S(1)}, u32[]{:S(2)}, u32[]{:S(2)}) %collective-permute-start.2) | collective-permute-done | bytes 131104 | tf_op jit(solution)/shard_map/ppermute | solution.py:342
  31.2 2.2 %collective-permute-start.5 = (bf16[128,512]{1,0:T(8,128)(2,1)S(1)}, bf16[128,512]{1,0:T(8,128)(2,1)S(1)}, u32[]{:S(2)}, u32[]{:S(2)}) collective-permute-start(bf16[128,512]{1,0:T(8,128)(2,1)S(1)} %copy-done.4), channel_id=1, source_target_pairs={{0,16},{2,18},{8,24},{10,26},{16,0},{18,2},{24,8},{26,10},{1,17},{... | collective-permute-start | bytes 393224 | tf_op jit(solution)/shard_map/ppermute | solution.py:342
  33.5 2.1 %collective-permute-start.6 = (bf16[128,512]{1,0:T(8,128)(2,1)S(1)}, bf16[128,512]{1,0:T(8,128)(2,1)S(1)}, u32[]{:S(2)}, u32[]{:S(2)}) collective-permute-start(bf16[128,512]{1,0:T(8,128)(2,1)S(1)} %copy-done.3), channel_id=1, source_target_pairs={{0,18},{2,16},{8,26},{10,24},{16,2},{18,0},{24,10},{26,8},{1,19},{... | collective-permute-start | bytes 393224 | tf_op jit(solution)/shard_map/ppermute | solution.py:342
  35.6 1.3 %broadcast_multiply_fusion.cache_ref = bf16[8,2,256,128]{3,2,1,0:T(8,128)(2,1)S(1)} fusion(bf16[8,2,256,128]{3,2,1,0:T(8,128)(2,1)} %turn_cache.1, bf16[2,256,128]{2,1,0:T(8,128)(2,1)S(1)} %pad_maximum_fusion), kind=kLoop, calls=%fused_computation.2 | loop fusion | flops 524288 | bytes 2228224 | tf_op jit(solution)/shard_map/mul | solution.py:353
  37.1 2.3 %attend.7 = (bf16[128,512]{1,0:T(8,128)(2,1)S(1)}, bf16[128,512]{1,0:T(8,128)(2,1)S(1)}) custom-call(s32[4]{0:T(128)S(1)} %copy-done.1, s32[32]{0:T(128)S(1)} %copy-done.2, s32[32]{0:T(128)S(1)} %convert_reduce_fusion.firsts, bf16[128,512]{1,0:T(8,128)(2,1)S(1)} %copy-done, bf16[128,512]{1,0:T(8,128)(2,1)S(1)} %collective-permute-done.q1_ref, ...), custom_call_target="tpu_custom_call" | custom-call | flops 805306368 | bytes 524288 | tf_op jit(solution)/shard_map/attend/pallas_call | solution.py:258
  39.4 2.0 %collective-permute-start.14 = (bf16[128,512]{1,0:T(8,128)(2,1)S(1)}, bf16[128,512]{1,0:T(8,128)(2,1)S(1)}, u32[]{:S(2)}, u32[]{:S(2)}) collective-permute-start(bf16[128,512]{1,0:T(8,128)(2,1)S(1)} %get-tuple-element.69), channel_id=1, source_target_pairs={{0,32},{2,34},{8,40},{10,42},{16,48},{18,50},{24,56},{26,58},{32,6... | collective-permute-start | bytes 393224 | tf_op jit(solution)/shard_map/ppermute | solution.py:371
  41.4 2.1 %collective-permute-start.15 = (bf16[128,512]{1,0:T(8,128)(2,1)S(1)}, bf16[128,512]{1,0:T(8,128)(2,1)S(1)}, u32[]{:S(2)}, u32[]{:S(2)}) collective-permute-start(bf16[128,512]{1,0:T(8,128)(2,1)S(1)} %get-tuple-element.70), channel_id=1, source_target_pairs={{0,34},{2,32},{8,42},{10,40},{16,50},{18,48},{24,58},{26,56},{32,6... | collective-permute-start | bytes 393224 | tf_op jit(solution)/shard_map/ppermute | solution.py:371
  43.5 3.5 %attend.6 = (bf16[128,512]{1,0:T(8,128)(2,1)S(1)}, bf16[128,512]{1,0:T(8,128)(2,1)S(1)}) custom-call(s32[4]{0:T(128)S(1)} %copy-done.1, s32[32]{0:T(128)S(1)} %copy-done.2, s32[32]{0:T(128)S(1)} %convert_reduce_fusion.firsts, bf16[128,512]{1,0:T(8,128)(2,1)S(1)} %collective-permute-done.1.q0_ref, bf16[128,512]{1,0:T(8,128)(2,1)S(1)} %collective-permute-done.2.q1_ref, ...), custom_call_target="tpu_custom_call" | custom-call | flops 805306368 | bytes 524288 | tf_op jit(solution)/shard_map/attend/pallas_call | solution.py:258
  46.9 1.8 %attend.5 = (bf16[128,512]{1,0:T(8,128)(2,1)S(1)}, bf16[128,512]{1,0:T(8,128)(2,1)S(1)}) custom-call(s32[4]{0:T(128)S(1)} %copy-done.1, s32[32]{0:T(128)S(1)} %copy-done.2, s32[32]{0:T(128)S(1)} %convert_reduce_fusion.firsts, bf16[128,512]{1,0:T(8,128)(2,1)S(1)} %collective-permute-done.3.q0_ref, bf16[128,512]{1,0:T(8,128)(2,1)S(1)} %collective-permute-done.4.q1_ref, ...), custom_call_target="tpu_custom_call" | custom-call | flops 805306368 | bytes 524288 | tf_op jit(solution)/shard_map/attend/pallas_call | solution.py:258
  48.8 5.4 %attend.4 = (bf16[128,512]{1,0:T(8,128)(2,1)S(1)}, bf16[128,512]{1,0:T(8,128)(2,1)S(1)}) custom-call(s32[4]{0:T(128)S(1)} %copy-done.1, s32[32]{0:T(128)S(1)} %copy-done.2, s32[32]{0:T(128)S(1)} %convert_reduce_fusion.firsts, bf16[128,512]{1,0:T(8,128)(2,1)S(1)} %collective-permute-done.5.q0_ref, bf16[128,512]{1,0:T(8,128)(2,1)S(1)} %collective-permute-done.6.q1_ref, ...), custom_call_target="tpu_custom_call" | custom-call | flops 805306368 | bytes 524288 | tf_op jit(solution)/shard_map/attend/pallas_call | solution.py:258
  54.2 3.6 %collective-permute-start.10 = (bf16[128,512]{1,0:T(8,128)(2,1)S(1)}, bf16[128,512]{1,0:T(8,128)(2,1)S(1)}, u32[]{:S(2)}, u32[]{:S(2)}) collective-permute-start(bf16[128,512]{1,0:T(8,128)(2,1)S(1)} %get-tuple-element.63), channel_id=1, source_target_pairs={{0,48},{2,50},{8,56},{10,58},{16,32},{18,34},{24,40},{26,42},{32,8... | collective-permute-start | bytes 393224 | tf_op jit(solution)/shard_map/ppermute | solution.py:371
  57.8 4.7 %collective-permute-start.11 = (bf16[128,512]{1,0:T(8,128)(2,1)S(1)}, bf16[128,512]{1,0:T(8,128)(2,1)S(1)}, u32[]{:S(2)}, u32[]{:S(2)}) collective-permute-start(bf16[128,512]{1,0:T(8,128)(2,1)S(1)} %get-tuple-element.64), channel_id=1, source_target_pairs={{0,50},{2,48},{8,58},{10,56},{16,34},{18,32},{24,42},{26,40},{32,8... | collective-permute-start | bytes 393224 | tf_op jit(solution)/shard_map/ppermute | solution.py:371
  62.5 1.7 %collective-permute-start.12 = (bf16[128,512]{1,0:T(8,128)(2,1)S(1)}, bf16[128,512]{1,0:T(8,128)(2,1)S(1)}, u32[]{:S(2)}, u32[]{:S(2)}) collective-permute-start(bf16[128,512]{1,0:T(8,128)(2,1)S(1)} %get-tuple-element.65), channel_id=1, source_target_pairs={{0,56},{2,58},{8,32},{10,34},{16,40},{18,42},{24,48},{26,50},{32,8... | collective-permute-start | bytes 393224 | tf_op jit(solution)/shard_map/ppermute | solution.py:371
  64.1 2.7 %collective-permute-start.13 = (bf16[128,512]{1,0:T(8,128)(2,1)S(1)}, bf16[128,512]{1,0:T(8,128)(2,1)S(1)}, u32[]{:S(2)}, u32[]{:S(2)}) collective-permute-start(bf16[128,512]{1,0:T(8,128)(2,1)S(1)} %get-tuple-element.66), channel_id=1, source_target_pairs={{0,58},{2,56},{8,34},{10,32},{16,42},{18,40},{24,50},{26,48},{32,9... | collective-permute-start | bytes 393224 | tf_op jit(solution)/shard_map/ppermute | solution.py:371
  67.4 1.1 %collective-permute-start.9 = (bf16[128,512]{1,0:T(8,128)(2,1)S(1)}, bf16[128,512]{1,0:T(8,128)(2,1)S(1)}, u32[]{:S(2)}, u32[]{:S(2)}) collective-permute-start(bf16[128,512]{1,0:T(8,128)(2,1)S(1)} %get-tuple-element.62), channel_id=1, source_target_pairs={{0,42},{2,40},{8,50},{10,48},{16,58},{18,56},{24,34},{26,32},{32,7... | collective-permute-start | bytes 393224 | tf_op jit(solution)/shard_map/ppermute | solution.py:371
  68.5 1.3 %join.3.refs_4_ = bf16[128,4096]{1,0:T(8,128)(2,1)} custom-call(s32[4]{0:T(128)S(1)} %copy-done.1, bf16[128,512]{1,0:T(8,128)(2,1)S(1)} %collective-permute-done.14.refs_0_, bf16[128,512]{1,0:T(8,128)(2,1)S(1)} %collective-permute-done.15.refs_1_), custom_call_target="tpu_custom_call" | custom-call | tf_op jit(solution)/shard_map/join/pallas_call | solution.py:300
  69.8 1.4 %collective-permute-done.12.refs_2_ = bf16[128,512]{1,0:T(8,128)(2,1)S(1)} collective-permute-done((bf16[128,512]{1,0:T(8,128)(2,1)S(1)}, bf16[128,512]{1,0:T(8,128)(2,1)S(1)}, u32[]{:S(2)}, u32[]{:S(2)}) %collective-permute-start.12) | collective-permute-done | bytes 131104 | tf_op jit(solution)/shard_map/ppermute | solution.py:371
  71.1 2.7 %collective-permute-done.13.refs_3_ = bf16[128,512]{1,0:T(8,128)(2,1)S(1)} collective-permute-done((bf16[128,512]{1,0:T(8,128)(2,1)S(1)}, bf16[128,512]{1,0:T(8,128)(2,1)S(1)}, u32[]{:S(2)}, u32[]{:S(2)}) %collective-permute-start.13) | collective-permute-done | bytes 131104 | tf_op jit(solution)/shard_map/ppermute | solution.py:371
  73.8 1.4 %join.4.refs_2_ = bf16[128,4096]{1,0:T(8,128)(2,1)} custom-call(s32[4]{0:T(128)S(1)} %copy-done.1, bf16[128,512]{1,0:T(8,128)(2,1)S(1)} %collective-permute-done.10.refs_0_, bf16[128,512]{1,0:T(8,128)(2,1)S(1)} %collective-permute-done.11.refs_1_, bf16[128,512]{1,0:T(8,128)(2,1)S(1)} %collective-permute-done.12.refs_2_, ...), custom_call_target="tpu_custom_call", output_to_operand_aliasing={{}: (5, {})} | custom-call | tf_op jit(solution)/shard_map/join/pallas_call | solution.py:300
  75.2 2.5 %collective-permute-done.8.refs_0_ = bf16[128,512]{1,0:T(8,128)(2,1)S(1)} collective-permute-done((bf16[128,512]{1,0:T(8,128)(2,1)S(1)}, bf16[128,512]{1,0:T(8,128)(2,1)S(1)}, u32[]{:S(2)}, u32[]{:S(2)}) %collective-permute-start.8) | collective-permute-done | bytes 131104 | tf_op jit(solution)/shard_map/ppermute | solution.py:371
  77.6 1.8 %collective-permute-done.9.refs_1_ = bf16[128,512]{1,0:T(8,128)(2,1)S(1)} collective-permute-done((bf16[128,512]{1,0:T(8,128)(2,1)S(1)}, bf16[128,512]{1,0:T(8,128)(2,1)S(1)}, u32[]{:S(2)}, u32[]{:S(2)}) %collective-permute-start.9) | collective-permute-done | bytes 131104 | tf_op jit(solution)/shard_map/ppermute | solution.py:371
  79.4 1.3 %join.5 = bf16[128,4096]{1,0:T(8,128)(2,1)} custom-call(s32[4]{0:T(128)S(1)} %copy-done.1, bf16[128,512]{1,0:T(8,128)(2,1)S(1)} %collective-permute-done.8.refs_0_, bf16[128,512]{1,0:T(8,128)(2,1)S(1)} %collective-permute-done.9.refs_1_, bf16[128,4096]{1,0:T(8,128)(2,1)} %join.4.refs_2_), custom_call_target="tpu_custom_call", output_to_operand_aliasing={{}: (3, {})} | custom-call | tf_op jit(solution)/shard_map/join/pallas_call | solution.py:300
  (32 shorter events, 2.3 us)
Async XLA Ops:
  2.0 28.9 %all-to-all-start = ((bf16[32,128,128]{2,1,0:T(8,128)(2,1)}), bf16[32,128,128]{2,1,0:T(8,128)(2,1)S(1)}, u32[]{:S(2)}, u32[]{:S(2)}) async-start(bf16[32,128,128]{2,1,0:T(8,128)(2,1)} %bitcast.15), calls=%async_computation | async-start | bytes 2097152 | tf_op jit(solution)/shard_map/all_to_all | solution.py:338
  13.0 12.8 %collective-permute-start = (bf16[128,512]{1,0:T(8,128)(2,1)}, bf16[128,512]{1,0:T(8,128)(2,1)S(1)}, u32[]{:S(2)}, u32[]{:S(2)}) collective-permute-start(bf16[128,512]{1,0:T(8,128)(2,1)} %get-tuple-element.39), channel_id=1, source_target_pairs={{0,2},{2,0},{8,10},{10,8},{16,18},{18,16},{24,26},{26,24},{1,3},{3... | collective-permute-start | bytes 393224 | tf_op jit(solution)/shard_map/ppermute | solution.py:342
  13.9 12.5 %collective-permute-start.1 = (bf16[128,512]{1,0:T(8,128)(2,1)}, bf16[128,512]{1,0:T(8,128)(2,1)S(1)}, u32[]{:S(2)}, u32[]{:S(2)}) collective-permute-start(bf16[128,512]{1,0:T(8,128)(2,1)} %get-tuple-element.40), channel_id=1, source_target_pairs={{0,24},{2,26},{8,0},{10,2},{16,8},{18,10},{24,16},{26,18},{1,25},{... | collective-permute-start | bytes 393224 | tf_op jit(solution)/shard_map/ppermute | solution.py:342
  14.4 16.5 %collective-permute-start.2 = (bf16[128,512]{1,0:T(8,128)(2,1)}, bf16[128,512]{1,0:T(8,128)(2,1)S(1)}, u32[]{:S(2)}, u32[]{:S(2)}) collective-permute-start(bf16[128,512]{1,0:T(8,128)(2,1)} %get-tuple-element.41), channel_id=1, source_target_pairs={{0,26},{2,24},{8,2},{10,0},{16,10},{18,8},{24,18},{26,16},{1,27},{... | collective-permute-start | bytes 393224 | tf_op jit(solution)/shard_map/ppermute | solution.py:342
  17.8 13.1 %collective-permute-start.3 = (bf16[128,512]{1,0:T(8,128)(2,1)}, bf16[128,512]{1,0:T(8,128)(2,1)S(1)}, u32[]{:S(2)}, u32[]{:S(2)}) collective-permute-start(bf16[128,512]{1,0:T(8,128)(2,1)} %get-tuple-element.44), channel_id=1, source_target_pairs={{0,8},{2,10},{8,16},{10,18},{16,24},{18,26},{24,0},{26,2},{1,9},{3... | collective-permute-start | bytes 393224 | tf_op jit(solution)/shard_map/ppermute | solution.py:342
  17.8 13.1 %collective-permute-start.4 = (bf16[128,512]{1,0:T(8,128)(2,1)}, bf16[128,512]{1,0:T(8,128)(2,1)S(1)}, u32[]{:S(2)}, u32[]{:S(2)}) collective-permute-start(bf16[128,512]{1,0:T(8,128)(2,1)} %get-tuple-element.45), channel_id=1, source_target_pairs={{0,10},{2,8},{8,18},{10,16},{16,26},{18,24},{24,2},{26,0},{1,11},{... | collective-permute-start | bytes 393224 | tf_op jit(solution)/shard_map/ppermute | solution.py:342
  19.5 11.5 %copy-start.2 = (s32[32]{0:T(128)S(1)}, s32[32]{0:T(128)}, u32[]{:S(2)}) copy-start(s32[32]{0:T(128)} %docs.7) | copy-start | bytes 388
  19.5 11.7 %copy-start.4 = (bf16[128,512]{1,0:T(8,128)(2,1)S(1)}, bf16[128,512]{1,0:T(8,128)(2,1)}, u32[]{:S(2)}) copy-start(bf16[128,512]{1,0:T(8,128)(2,1)} %get-tuple-element.46) | copy-start | bytes 393220
  19.5 13.9 %copy-start.3 = (bf16[128,512]{1,0:T(8,128)(2,1)S(1)}, bf16[128,512]{1,0:T(8,128)(2,1)}, u32[]{:S(2)}) copy-start(bf16[128,512]{1,0:T(8,128)(2,1)} %get-tuple-element.47) | copy-start | bytes 393220
  19.6 17.5 %copy-start = (bf16[128,512]{1,0:T(8,128)(2,1)S(1)}, bf16[128,512]{1,0:T(8,128)(2,1)}, u32[]{:S(2)}) copy-start(bf16[128,512]{1,0:T(8,128)(2,1)} %get-tuple-element.67.q0_ref) | copy-start | bytes 393220
  19.6 17.5 %copy-start.1 = (s32[4]{0:T(128)S(1)}, s32[4]{0:T(128)}, u32[]{:S(2)}) copy-start(s32[4]{0:T(128)} %pad_add_fusion.place) | copy-start | bytes 52
  30.9 6.0 %collective-permute-start.7 = (bf16[32,128,128]{2,1,0:T(8,128)(2,1)S(1)}, bf16[32,128,128]{2,1,0:T(8,128)(2,1)S(1)}, u32[]{:S(2)}, u32[]{:S(2)}) collective-permute-start(bf16[32,128,128]{2,1,0:T(8,128)(2,1)S(1)} %all-to-all-done), channel_id=1, source_target_pairs={{0,1},{1,0},{2,3},{3,2},{4,5},{5,4},{6,7},{7,6},{8,9},{9,8},{10,11... | collective-permute-start | bytes 3145736 | tf_op jit(solution)/shard_map/ppermute | solution.py:354
  31.2 17.5 %collective-permute-start.5 = (bf16[128,512]{1,0:T(8,128)(2,1)S(1)}, bf16[128,512]{1,0:T(8,128)(2,1)S(1)}, u32[]{:S(2)}, u32[]{:S(2)}) collective-permute-start(bf16[128,512]{1,0:T(8,128)(2,1)S(1)} %copy-done.4), channel_id=1, source_target_pairs={{0,16},{2,18},{8,24},{10,26},{16,0},{18,2},{24,8},{26,10},{1,17},{... | collective-permute-start | bytes 393224 | tf_op jit(solution)/shard_map/ppermute | solution.py:342
  33.5 15.3 %collective-permute-start.6 = (bf16[128,512]{1,0:T(8,128)(2,1)S(1)}, bf16[128,512]{1,0:T(8,128)(2,1)S(1)}, u32[]{:S(2)}, u32[]{:S(2)}) collective-permute-start(bf16[128,512]{1,0:T(8,128)(2,1)S(1)} %copy-done.3), channel_id=1, source_target_pairs={{0,18},{2,16},{8,26},{10,24},{16,2},{18,0},{24,10},{26,8},{1,19},{... | collective-permute-start | bytes 393224 | tf_op jit(solution)/shard_map/ppermute | solution.py:342
  39.4 24.8 %collective-permute-start.14 = (bf16[128,512]{1,0:T(8,128)(2,1)S(1)}, bf16[128,512]{1,0:T(8,128)(2,1)S(1)}, u32[]{:S(2)}, u32[]{:S(2)}) collective-permute-start(bf16[128,512]{1,0:T(8,128)(2,1)S(1)} %get-tuple-element.69), channel_id=1, source_target_pairs={{0,32},{2,34},{8,40},{10,42},{16,48},{18,50},{24,56},{26,58},{32,6... | collective-permute-start | bytes 393224 | tf_op jit(solution)/shard_map/ppermute | solution.py:371
  41.4 25.5 %collective-permute-start.15 = (bf16[128,512]{1,0:T(8,128)(2,1)S(1)}, bf16[128,512]{1,0:T(8,128)(2,1)S(1)}, u32[]{:S(2)}, u32[]{:S(2)}) collective-permute-start(bf16[128,512]{1,0:T(8,128)(2,1)S(1)} %get-tuple-element.70), channel_id=1, source_target_pairs={{0,34},{2,32},{8,42},{10,40},{16,50},{18,48},{24,58},{26,56},{32,6... | collective-permute-start | bytes 393224 | tf_op jit(solution)/shard_map/ppermute | solution.py:371
  54.2 13.2 %collective-permute-start.10 = (bf16[128,512]{1,0:T(8,128)(2,1)S(1)}, bf16[128,512]{1,0:T(8,128)(2,1)S(1)}, u32[]{:S(2)}, u32[]{:S(2)}) collective-permute-start(bf16[128,512]{1,0:T(8,128)(2,1)S(1)} %get-tuple-element.63), channel_id=1, source_target_pairs={{0,48},{2,50},{8,56},{10,58},{16,32},{18,34},{24,40},{26,42},{32,8... | collective-permute-start | bytes 393224 | tf_op jit(solution)/shard_map/ppermute | solution.py:371
  57.8 12.0 %collective-permute-start.11 = (bf16[128,512]{1,0:T(8,128)(2,1)S(1)}, bf16[128,512]{1,0:T(8,128)(2,1)S(1)}, u32[]{:S(2)}, u32[]{:S(2)}) collective-permute-start(bf16[128,512]{1,0:T(8,128)(2,1)S(1)} %get-tuple-element.64), channel_id=1, source_target_pairs={{0,50},{2,48},{8,58},{10,56},{16,34},{18,32},{24,42},{26,40},{32,8... | collective-permute-start | bytes 393224 | tf_op jit(solution)/shard_map/ppermute | solution.py:371
  62.5 8.7 %collective-permute-start.12 = (bf16[128,512]{1,0:T(8,128)(2,1)S(1)}, bf16[128,512]{1,0:T(8,128)(2,1)S(1)}, u32[]{:S(2)}, u32[]{:S(2)}) collective-permute-start(bf16[128,512]{1,0:T(8,128)(2,1)S(1)} %get-tuple-element.65), channel_id=1, source_target_pairs={{0,56},{2,58},{8,32},{10,34},{16,40},{18,42},{24,48},{26,50},{32,8... | collective-permute-start | bytes 393224 | tf_op jit(solution)/shard_map/ppermute | solution.py:371
  64.1 9.7 %collective-permute-start.13 = (bf16[128,512]{1,0:T(8,128)(2,1)S(1)}, bf16[128,512]{1,0:T(8,128)(2,1)S(1)}, u32[]{:S(2)}, u32[]{:S(2)}) collective-permute-start(bf16[128,512]{1,0:T(8,128)(2,1)S(1)} %get-tuple-element.66), channel_id=1, source_target_pairs={{0,58},{2,56},{8,34},{10,32},{16,42},{18,40},{24,50},{26,48},{32,9... | collective-permute-start | bytes 393224 | tf_op jit(solution)/shard_map/ppermute | solution.py:371
  66.8 10.8 %collective-permute-start.8 = (bf16[128,512]{1,0:T(8,128)(2,1)S(1)}, bf16[128,512]{1,0:T(8,128)(2,1)S(1)}, u32[]{:S(2)}, u32[]{:S(2)}) collective-permute-start(bf16[128,512]{1,0:T(8,128)(2,1)S(1)} %get-tuple-element.61), channel_id=1, source_target_pairs={{0,40},{2,42},{8,48},{10,50},{16,56},{18,58},{24,32},{26,34},{32,7... | collective-permute-start | bytes 393224 | tf_op jit(solution)/shard_map/ppermute | solution.py:371
  67.4 12.0 %collective-permute-start.9 = (bf16[128,512]{1,0:T(8,128)(2,1)S(1)}, bf16[128,512]{1,0:T(8,128)(2,1)S(1)}, u32[]{:S(2)}, u32[]{:S(2)}) collective-permute-start(bf16[128,512]{1,0:T(8,128)(2,1)S(1)} %get-tuple-element.62), channel_id=1, source_target_pairs={{0,42},{2,40},{8,50},{10,48},{16,58},{18,56},{24,34},{26,32},{32,7... | collective-permute-start | bytes 393224 | tf_op jit(solution)/shard_map/ppermute | solution.py:371
